TPU v7x, 32 devices: a whole 2x2x4 slice. The times are simulated.
32 devices in a mesh: section: 2 (over x), dp: 16 (over z, y, core).
Axes of the slice: x: 2, y: 2, z: 4, core: 2. Of those that a mesh axis runs over, the one named last changes fastest.
Arguments:
- ends: bfloat16 [2, 16384, 512], P('section', 'dp'), may hold values from -6 to 6
- lengths: int32 [32], P('dp'), may hold values from 144 to 512, as said below
- seg_group: int32 [32], P('dp'), may hold values from 0 to 1
- norm_gain: float32 [2, 3, 512], P('section'), may hold values from 0.5 to 1.5
- norm_shift: float32 [2, 3, 512], P('section'), may hold values from -1 to 1
- w_query: bfloat16 [2, 512, 512], P('section'), may hold values from -0.25 to 0.25
- w_key: bfloat16 [2, 512, 512], P('section'), may hold values from -0.25 to 0.25
- w_value: bfloat16 [2, 512, 512], P('section'), may hold values from -0.25 to 0.25
- qv_bias: float32 [2, 2, 512], P('section'), may hold values from -1.5 to 1.5
- w_out: bfloat16 [2, 512, 512], P('section'), may hold values from -0.75 to 0.75
- out_bias: float32 [2, 512], P('section'), may hold values from -1.5 to 1.5
- w_up: bfloat16 [2, 512, 2048], P('section'), may hold values from -0.25 to 0.25
- up_bias: float32 [2, 2048], P('section'), may hold values from -2.5 to 2.5
- w_down: bfloat16 [2, 2048, 512], P('section'), may hold values from -0.125 to 0.125
- down_bias: float32 [2, 512], P('section'), may hold values from -1.5 to 1.5
Outputs:
- ends_out: bfloat16 [2, 16384, 512], P('section', 'dp')
- grad_norm_gain: float32 [2, 3, 512], P('section')
- grad_norm_shift: float32 [2, 3, 512], P('section')
- grad_w_query: float32 [2, 512, 512], P('section')
- grad_w_key: float32 [2, 512, 512], P('section')
- grad_w_value: float32 [2, 512, 512], P('section')
- grad_qv_bias: float32 [2, 2, 512], P('section')
- grad_w_out: float32 [2, 512, 512], P('section')
- grad_out_bias: float32 [2, 512], P('section')
- grad_w_up: float32 [2, 512, 2048], P('section')
- grad_up_bias: float32 [2, 2048], P('section')
- grad_w_down: float32 [2, 2048, 512], P('section')
- grad_down_bias: float32 [2, 512], P('section')
Inputs may be any that keep to these rules, and one draw needn't show every extreme that they name: `lengths`: frames of each utterance; in every draw one utterance has exactly 512 frames and one exactly 144.
All inputs are finite; a program needn't handle non-finite values.
Results may differ from a plain program's by a relative error of at most 0.02.
Values may be sent and summed in bfloat16 or wider, within the bound.
No kernel may reach another device: no remote copies, remote signals or barrier semaphores. Data moves between devices by JAX's collectives and lax.ppermute only.
A program may use at most 256 MiB of HBM per device.

v0:
```python
import jax
import jax.numpy as jnp
from jax import lax
from jax.sharding import PartitionSpec as P

H = 8
E = 64
BLOCK = 512
TILE = 128
LEFT = 30
RIGHT = 4
MEM = 4
MB = 2


def shifted(block, axis, distance):
    devices = range(lax.axis_size(axis))
    route = [(i - distance, i) for i in devices if i - distance in devices]
    return lax.ppermute(block, axis, route)


def norm_rows(value, gain, shift):
    center = value - jnp.mean(value, axis=-1, keepdims=True)
    spread = jnp.mean(center * center, axis=-1, keepdims=True)
    return center * lax.rsqrt(spread + 1e-05) * gain + shift


def segment_means(value, length, wide):
    rows = value.shape[0] // 8
    width = value.shape[1]
    eight = jnp.sum(value.reshape(rows, 8, width), axis=1)
    sixteen = jnp.sum(value.reshape(rows // 2, 16, width), axis=1)
    sixteen = jnp.concatenate([sixteen, jnp.zeros((rows // 2, width), value.dtype)], axis=0)
    totals = jnp.where(wide, sixteen, eight)
    segment = jnp.where(wide, 16, 8).astype(jnp.int32)
    count = jnp.clip(length - jnp.arange(rows, dtype=jnp.int32) * segment, 0, segment)
    return totals / jnp.maximum(count, 1).astype(value.dtype)[:, None]


def segment_spread(value, length, wide):
    rows, width = value.shape
    segment = jnp.where(wide, 16, 8).astype(jnp.int32)
    count = jnp.clip(length - jnp.arange(rows, dtype=jnp.int32) * segment, 0, segment)
    scaled = value / jnp.maximum(count, 1).astype(jnp.float32)[:, None]
    eight = jnp.broadcast_to(scaled[:, None, :], (rows, 8, width)).reshape(rows * 8, width)
    sixteen = jnp.broadcast_to(scaled[: rows // 2, None, :], (rows // 2, 16, width)).reshape(
        rows * 8, width
    )
    valid = (jnp.arange(rows * 8, dtype=jnp.int32) < length).astype(jnp.float32)[:, None]
    return jnp.where(wide, sixteen, eight) * valid


def tile_mask(block, length, wide):
    tiles = BLOCK // TILE
    rows_summary = TILE // 8
    segment = jnp.where(wide, 16, 8).astype(jnp.int32)
    anchor = block * BLOCK + jnp.arange(tiles, dtype=jnp.int32) * TILE
    frames = anchor[:, None] + jnp.arange(TILE, dtype=jnp.int32)[None, :]
    start = anchor // segment
    summary_index = start[:, None] + jnp.arange(rows_summary, dtype=jnp.int32)[None, :]
    query_segment = jnp.concatenate([frames // segment, summary_index], axis=1)
    is_frame = jnp.arange(TILE + rows_summary, dtype=jnp.int32) < TILE
    key_frame = anchor[:, None] - 32 + jnp.arange(TILE + 64, dtype=jnp.int32)[None, :]
    lower = (query_segment * segment - LEFT)[:, :, None]
    upper = (query_segment * segment + segment + RIGHT)[:, :, None]
    key_here = key_frame[:, None, :]
    frame_ok = (key_here >= lower) & (key_here < upper) & (key_here < length) & (key_here >= 0)
    memory_index = (start[:, None] - 8 + jnp.arange(rows_summary + 16, dtype=jnp.int32)[None, :])[
        :, None, :
    ]
    memory_ok = (memory_index >= query_segment[:, :, None] - MEM) & (
        memory_index < query_segment[:, :, None]
    )
    memory_ok = memory_ok & (memory_index >= 0) & is_frame[None, :, None]
    summary_ok = jnp.arange(rows_summary, dtype=jnp.int32) < TILE // segment
    return (jnp.concatenate([memory_ok, frame_ok], axis=2), start, summary_ok)


def padded_sources(table, mem_rows):
    return (
        jnp.pad(table[:mem_rows], ((8, 16), (0, 0))),
        jnp.pad(table[mem_rows:], ((32, 32), (0, 0))),
    )


def tile_operands(block, query_frames, query_summary, key_parts, value_parts, start):
    rows_summary = TILE // 8
    queries = []
    keys = []
    values = []
    for tile in range(BLOCK // TILE):
        anchor = block * BLOCK + tile * TILE
        queries.append(
            jnp.concatenate(
                [
                    query_frames[anchor : anchor + TILE],
                    lax.dynamic_slice_in_dim(query_summary, start[tile], rows_summary, 0),
                ],
                axis=0,
            )
        )
        keys.append(
            jnp.concatenate(
                [
                    lax.dynamic_slice_in_dim(key_parts[0], start[tile], rows_summary + 16, 0),
                    key_parts[1][anchor : anchor + TILE + 64],
                ],
                axis=0,
            )
        )
        values.append(
            jnp.concatenate(
                [
                    lax.dynamic_slice_in_dim(value_parts[0], start[tile], rows_summary + 16, 0),
                    value_parts[1][anchor : anchor + TILE + 64],
                ],
                axis=0,
            )
        )
    tiles = BLOCK // TILE
    return (
        jnp.stack(queries).reshape(tiles, -1, H, E),
        jnp.stack(keys).reshape(tiles, -1, H, E),
        jnp.stack(values).reshape(tiles, -1, H, E),
    )


def fold_tiles(parts):
    width = parts.shape[2]
    center = parts[:, 32 : 32 + TILE]
    left_flap = parts[:, :32]
    right_flap = parts[:, 32 + TILE :]
    blank = jnp.zeros_like(left_flap[:1])
    tail = jnp.concatenate([left_flap[1:], blank], axis=0)
    head = jnp.concatenate([blank, right_flap[:-1]], axis=0)
    joined = (
        center
        + jnp.pad(head, ((0, 0), (0, TILE - 32), (0, 0)))
        + jnp.pad(tail, ((0, 0), (TILE - 32, 0), (0, 0)))
    )
    return joined.reshape(-1, width)


def attend_forward(query_frames, query_summary, keys, values, length, wide):
    slot_len, width = query_frames.shape
    mem_rows = slot_len // 8
    scale = E ** (-0.5)
    tiles = BLOCK // TILE
    key_parts = padded_sources(keys, mem_rows)
    value_parts = padded_sources(values, mem_rows)
    out_frames = []
    log_totals = []
    out_summary = jnp.zeros((mem_rows, width), jnp.float32)
    for block in range(slot_len // BLOCK):
        mask, start, summary_ok = tile_mask(block, length, wide)
        query, key, value = tile_operands(
            block, query_frames, query_summary, key_parts, value_parts, start
        )
        scores = (
            jnp.einsum("nrhe,nkhe->nhrk", query, key, preferred_element_type=jnp.float32) * scale
        )
        scores = jnp.where(mask[:, None], scores, -1e30)
        peak = jnp.max(scores, axis=-1, keepdims=True)
        expo = jnp.exp(scores - peak)
        total = jnp.sum(expo, axis=-1, keepdims=True)
        chance = (expo / total).astype(jnp.bfloat16)
        log_totals.append((peak + jnp.log(total))[..., 0])
        mixed = jnp.einsum(
            "nhrk,nkhe->nrhe", chance, value, preferred_element_type=jnp.float32
        ).reshape(tiles, -1, width)
        out_frames.append(mixed[:, :TILE].reshape(-1, width))
        for tile in range(tiles):
            placed = jnp.where(summary_ok[:, None], mixed[tile, TILE:], 0.0)
            out_summary = out_summary + lax.dynamic_update_slice_in_dim(
                jnp.zeros((mem_rows, width), jnp.float32), placed, start[tile], 0
            )
    return (jnp.concatenate(out_frames, axis=0), out_summary, jnp.stack(log_totals))


def attend_backward(
    query_frames, query_summary, keys, values, log_totals, grad_frames, grad_summary, length, wide
):
    slot_len, width = query_frames.shape
    mem_rows = slot_len // 8
    scale = E ** (-0.5)
    tiles = BLOCK // TILE
    rows_summary = TILE // 8
    memory_span = rows_summary + 16
    key_parts = padded_sources(keys, mem_rows)
    value_parts = padded_sources(values, mem_rows)
    grad_query_frames = []
    grad_query_summary = jnp.zeros((mem_rows, width), jnp.float32)
    grad_key_memory = jnp.zeros((mem_rows + 24, width), jnp.float32)
    grad_value_memory = jnp.zeros((mem_rows + 24, width), jnp.float32)
    key_frame_parts = []
    value_frame_parts = []
    for block in range(slot_len // BLOCK):
        mask, start, summary_ok = tile_mask(block, length, wide)
        query, key, value = tile_operands(
            block, query_frames, query_summary, key_parts, value_parts, start
        )
        scores = (
            jnp.einsum("nrhe,nkhe->nhrk", query, key, preferred_element_type=jnp.float32) * scale
        )
        scores = jnp.where(mask[:, None], scores, -1e30)
        chance_full = jnp.exp(scores - log_totals[block][..., None])
        chance_low = chance_full.astype(jnp.bfloat16)
        grad_pieces = []
        for tile in range(tiles):
            anchor = block * BLOCK + tile * TILE
            summary_grad = lax.dynamic_slice_in_dim(grad_summary, start[tile], rows_summary, 0)
            summary_grad = jnp.where(
                summary_ok[:, None], summary_grad, jnp.zeros_like(summary_grad)
            )
            grad_pieces.append(
                jnp.concatenate([grad_frames[anchor : anchor + TILE], summary_grad], axis=0)
            )
        grad_block = jnp.stack(grad_pieces).reshape(tiles, -1, H, E)
        grad_chance = jnp.einsum(
            "nrhe,nkhe->nhrk", grad_block, value, preferred_element_type=jnp.float32
        )
        inner = jnp.sum(chance_full * grad_chance, axis=-1, keepdims=True)
        grad_scores = (chance_full * (grad_chance - inner)).astype(jnp.bfloat16)
        grad_query = (
            jnp.einsum("nhrk,nkhe->nrhe", grad_scores, key, preferred_element_type=jnp.float32)
            * scale
        ).reshape(tiles, -1, width)
        grad_key = (
            jnp.einsum("nhrk,nrhe->nkhe", grad_scores, query, preferred_element_type=jnp.float32)
            * scale
        ).reshape(tiles, -1, width)
        grad_value = jnp.einsum(
            "nhrk,nrhe->nkhe", chance_low, grad_block, preferred_element_type=jnp.float32
        ).reshape(tiles, -1, width)
        grad_query_frames.append(grad_query[:, :TILE].reshape(-1, width))
        key_frame_parts.append(grad_key[:, memory_span:])
        value_frame_parts.append(grad_value[:, memory_span:])
        for tile in range(tiles):
            placed = jnp.where(summary_ok[:, None], grad_query[tile, TILE:], 0.0)
            grad_query_summary = grad_query_summary + lax.dynamic_update_slice_in_dim(
                jnp.zeros((mem_rows, width), jnp.float32), placed, start[tile], 0
            )
            current = lax.dynamic_slice_in_dim(grad_key_memory, start[tile], memory_span, 0)
            grad_key_memory = lax.dynamic_update_slice_in_dim(
                grad_key_memory, current + grad_key[tile, :memory_span], start[tile], 0
            )
            current = lax.dynamic_slice_in_dim(grad_value_memory, start[tile], memory_span, 0)
            grad_value_memory = lax.dynamic_update_slice_in_dim(
                grad_value_memory, current + grad_value[tile, :memory_span], start[tile], 0
            )
    grad_key_frames = fold_tiles(jnp.concatenate(key_frame_parts, axis=0))
    grad_value_frames = fold_tiles(jnp.concatenate(value_frame_parts, axis=0))
    grad_keys = jnp.concatenate([grad_key_memory[8 : 8 + mem_rows], grad_key_frames], axis=0)
    grad_values = jnp.concatenate([grad_value_memory[8 : 8 + mem_rows], grad_value_frames], axis=0)
    return (jnp.concatenate(grad_query_frames, axis=0), grad_query_summary, grad_keys, grad_values)


def frame_valid(length, slot_len):
    return (jnp.arange(slot_len, dtype=jnp.int32)[None, :] < length[:, None]).astype(jnp.float32)[
        ..., None
    ]


def layer_forward(weights, frames_in, memory_in, length, wide, first):
    (
        gain,
        shift,
        w_query,
        w_key,
        w_value,
        qv_bias,
        w_out,
        out_bias,
        w_up,
        up_bias,
        w_down,
        down_bias,
    ) = weights
    slot_len = frames_in.shape[1]
    inputs = frames_in.astype(jnp.float32)
    valid = frame_valid(length, slot_len)
    start_memory = jax.vmap(segment_means)(inputs * valid, length, wide).astype(jnp.bfloat16)
    memory = jnp.where(first, start_memory, memory_in)
    normed = norm_rows(inputs, gain[0], shift[0]).astype(jnp.bfloat16)
    summary = jax.vmap(segment_means)(normed.astype(jnp.float32) * valid, length, wide).astype(
        jnp.bfloat16
    )
    query_frames = (
        jnp.einsum("usd,de->use", normed, w_query, preferred_element_type=jnp.float32) + qv_bias[0]
    ).astype(jnp.bfloat16)
    query_summary = (
        jnp.einsum("usd,de->use", summary, w_query, preferred_element_type=jnp.float32) + qv_bias[0]
    ).astype(jnp.bfloat16)
    sources = jnp.concatenate([memory, normed], axis=1)
    keys = jnp.einsum("usd,de->use", sources, w_key, preferred_element_type=jnp.float32).astype(
        jnp.bfloat16
    )
    values = (
        jnp.einsum("usd,de->use", sources, w_value, preferred_element_type=jnp.float32) + qv_bias[1]
    ).astype(jnp.bfloat16)
    mixed_frames, mixed_summary, log_totals = jax.vmap(attend_forward)(
        query_frames, query_summary, keys, values, length, wide
    )
    mixed_frames = mixed_frames.astype(jnp.bfloat16)
    mixed_summary = mixed_summary.astype(jnp.bfloat16)
    branch_frames = (
        jnp.einsum("usd,de->use", mixed_frames, w_out, preferred_element_type=jnp.float32)
        + out_bias
    )
    branch_summary = (
        jnp.einsum("usd,de->use", mixed_summary, w_out, preferred_element_type=jnp.float32)
        + out_bias
    )
    after = inputs + branch_frames
    memory_out = branch_summary.astype(jnp.bfloat16)
    hidden_in = norm_rows(after, gain[1], shift[1]).astype(jnp.bfloat16)
    hidden = (
        jnp.einsum("usd,df->usf", hidden_in, w_up, preferred_element_type=jnp.float32) + up_bias
    )
    active = jax.nn.gelu(hidden, approximate=False).astype(jnp.bfloat16)
    after_ffn = (
        after
        + jnp.einsum("usf,fd->usd", active, w_down, preferred_element_type=jnp.float32)
        + down_bias
    )
    final = (norm_rows(after_ffn, gain[2], shift[2]) * valid).astype(jnp.bfloat16)
    kept = (
        frames_in,
        memory,
        normed,
        summary,
        query_frames,
        query_summary,
        keys,
        values,
        log_totals,
        mixed_frames,
        mixed_summary,
        after,
        hidden_in,
        active,
        after_ffn,
    )
    return (final, memory_out, kept)


def forward_blank(units, slot_len, width, hidden_width):
    mem_rows = slot_len // 8
    blocks = slot_len // BLOCK
    frames_bf = jnp.zeros((units, slot_len, width), jnp.bfloat16)
    memory_bf = jnp.zeros((units, mem_rows, width), jnp.bfloat16)
    sources_bf = jnp.zeros((units, mem_rows + slot_len, width), jnp.bfloat16)
    frames_fl = jnp.zeros((units, slot_len, width), jnp.float32)
    log_blank = jnp.zeros((units, blocks, BLOCK // TILE, H, TILE + TILE // 8), jnp.float32)
    kept = (
        frames_bf,
        memory_bf,
        frames_bf,
        memory_bf,
        frames_bf,
        memory_bf,
        sources_bf,
        sources_bf,
        log_blank,
        frames_bf,
        memory_bf,
        frames_fl,
        frames_bf,
        jnp.zeros((units, slot_len, hidden_width), jnp.bfloat16),
        frames_fl,
    )
    return (frames_bf, memory_bf, kept)


def ffn_blank(units, slot_len, width, hidden_width):
    terms = (
        jnp.zeros((2, width), jnp.float32),
        jnp.zeros((2, width), jnp.float32),
        jnp.zeros((width, hidden_width), jnp.float32),
        jnp.zeros((hidden_width,), jnp.float32),
        jnp.zeros((hidden_width, width), jnp.float32),
        jnp.zeros((width,), jnp.float32),
    )
    return (jnp.zeros((units, slot_len, width), jnp.float32), terms)


def attention_blank(units, slot_len, width):
    square = jnp.zeros((width, width), jnp.float32)
    terms = (
        jnp.zeros((1, width), jnp.float32),
        jnp.zeros((1, width), jnp.float32),
        square,
        square,
        square,
        jnp.zeros((2, width), jnp.float32),
        square,
        jnp.zeros((width,), jnp.float32),
    )
    return (
        jnp.zeros((units, slot_len, width), jnp.float32),
        jnp.zeros((units, slot_len // 8, width), jnp.float32),
        terms,
    )


def ffn_backward(weights, kept, grad_final, length):
    (
        gain,
        shift,
        w_query,
        w_key,
        w_value,
        qv_bias,
        w_out,
        out_bias,
        w_up,
        up_bias,
        w_down,
        down_bias,
    ) = weights
    after, hidden_in, active, after_ffn = (kept[11], kept[12], kept[13], kept[14])
    valid = frame_valid(length, after.shape[1])
    spare, back_top = jax.vjp(norm_rows, after_ffn, gain[2], shift[2])
    grad_after_ffn, grad_gain_top, grad_shift_top = back_top(grad_final.astype(jnp.float32) * valid)
    grad_update = grad_after_ffn.astype(jnp.bfloat16)
    grad_down = jnp.einsum("usf,usd->fd", active, grad_update, preferred_element_type=jnp.float32)
    grad_down_bias = jnp.sum(grad_update.astype(jnp.float32), axis=(0, 1))
    grad_active = jnp.einsum("usd,fd->usf", grad_update, w_down, preferred_element_type=jnp.float32)
    hidden = (
        jnp.einsum("usd,df->usf", hidden_in, w_up, preferred_element_type=jnp.float32) + up_bias
    )
    spare, gelu_back = jax.vjp(lambda value: jax.nn.gelu(value, approximate=False), hidden)
    grad_hidden = gelu_back(grad_active)[0].astype(jnp.bfloat16)
    grad_up = jnp.einsum("usd,usf->df", hidden_in, grad_hidden, preferred_element_type=jnp.float32)
    grad_up_bias = jnp.sum(grad_hidden.astype(jnp.float32), axis=(0, 1))
    grad_hidden_in = jnp.einsum(
        "usf,df->usd", grad_hidden, w_up, preferred_element_type=jnp.float32
    )
    spare, back_mid = jax.vjp(norm_rows, after, gain[1], shift[1])
    grad_after_norm, grad_gain_mid, grad_shift_mid = back_mid(grad_hidden_in)
    grad_after = grad_after_ffn + grad_after_norm
    terms = (
        jnp.stack([grad_gain_mid, grad_gain_top]),
        jnp.stack([grad_shift_mid, grad_shift_top]),
        grad_up,
        grad_up_bias,
        grad_down,
        grad_down_bias,
    )
    return (grad_after, terms)


def attention_backward(weights, kept, grad_after, grad_memory, length, wide, first):
    (
        gain,
        shift,
        w_query,
        w_key,
        w_value,
        qv_bias,
        w_out,
        out_bias,
        w_up,
        up_bias,
        w_down,
        down_bias,
    ) = weights
    (
        frames_in,
        memory,
        normed,
        summary,
        query_frames,
        query_summary,
        keys,
        values,
        log_totals,
        mixed_frames,
        mixed_summary,
    ) = kept[:11]
    mem_rows = memory.shape[1]
    grad_branch_frames = grad_after.astype(jnp.bfloat16)
    grad_out = jnp.einsum(
        "usd,use->de", mixed_frames, grad_branch_frames, preferred_element_type=jnp.float32
    )
    grad_out = grad_out + jnp.einsum(
        "usd,use->de", mixed_summary, grad_memory, preferred_element_type=jnp.float32
    )
    grad_out_bias = jnp.sum(grad_branch_frames.astype(jnp.float32), axis=(0, 1)) + jnp.sum(
        grad_memory.astype(jnp.float32), axis=(0, 1)
    )
    grad_mixed_frames = jnp.einsum(
        "use,de->usd", grad_branch_frames, w_out, preferred_element_type=jnp.float32
    ).astype(jnp.bfloat16)
    grad_mixed_summary = jnp.einsum(
        "use,de->usd", grad_memory, w_out, preferred_element_type=jnp.float32
    ).astype(jnp.bfloat16)
    grad_qf, grad_qs, grad_keys, grad_values = jax.vmap(attend_backward)(
        query_frames,
        query_summary,
        keys,
        values,
        log_totals,
        grad_mixed_frames,
        grad_mixed_summary,
        length,
        wide,
    )
    grad_qf = grad_qf.astype(jnp.bfloat16)
    grad_qs = grad_qs.astype(jnp.bfloat16)
    grad_keys = grad_keys.astype(jnp.bfloat16)
    grad_values = grad_values.astype(jnp.bfloat16)
    grad_w_query = jnp.einsum("usd,use->de", normed, grad_qf, preferred_element_type=jnp.float32)
    grad_w_query = grad_w_query + jnp.einsum(
        "usd,use->de", summary, grad_qs, preferred_element_type=jnp.float32
    )
    grad_query_bias = jnp.sum(grad_qf.astype(jnp.float32), axis=(0, 1)) + jnp.sum(
        grad_qs.astype(jnp.float32), axis=(0, 1)
    )
    sources = jnp.concatenate([memory, normed], axis=1)
    grad_w_key = jnp.einsum("usd,use->de", sources, grad_keys, preferred_element_type=jnp.float32)
    grad_w_value = jnp.einsum(
        "usd,use->de", sources, grad_values, preferred_element_type=jnp.float32
    )
    grad_value_bias = jnp.sum(grad_values.astype(jnp.float32), axis=(0, 1))
    grad_sources = jnp.einsum("use,de->usd", grad_keys, w_key, preferred_element_type=jnp.float32)
    grad_sources = grad_sources + jnp.einsum(
        "use,de->usd", grad_values, w_value, preferred_element_type=jnp.float32
    )
    grad_memory_in = grad_sources[:, :mem_rows]
    grad_normed = grad_sources[:, mem_rows:] + jnp.einsum(
        "use,de->usd", grad_qf, w_query, preferred_element_type=jnp.float32
    )
    grad_summary = jnp.einsum("use,de->usd", grad_qs, w_query, preferred_element_type=jnp.float32)
    grad_normed = grad_normed + jax.vmap(segment_spread)(grad_summary, length, wide)
    inputs = frames_in.astype(jnp.float32)
    spare, back_low = jax.vjp(norm_rows, inputs, gain[0], shift[0])
    grad_inputs_norm, grad_gain_low, grad_shift_low = back_low(grad_normed)
    pooled_back = jax.vmap(segment_spread)(grad_memory_in, length, wide)
    grad_inputs = grad_after + grad_inputs_norm + jnp.where(first, pooled_back, 0.0)
    terms = (
        grad_gain_low[None],
        grad_shift_low[None],
        grad_w_query,
        grad_w_key,
        grad_w_value,
        jnp.stack([grad_query_bias, grad_value_bias]),
        grad_out,
        grad_out_bias,
    )
    return (grad_inputs, grad_memory_in, terms)


def on_device(
    ends,
    lengths,
    seg_group,
    norm_gain,
    norm_shift,
    w_query,
    w_key,
    w_value,
    qv_bias,
    w_out,
    out_bias,
    w_up,
    up_bias,
    w_down,
    down_bias,
):
    weights = (
        norm_gain[0],
        norm_shift[0],
        w_query[0],
        w_key[0],
        w_value[0],
        qv_bias[0],
        w_out[0],
        out_bias[0],
        w_up[0],
        up_bias[0],
        w_down[0],
        down_bias[0],
    )
    section = lax.axis_index("section")
    first = section == 0
    slots = lengths.shape[0]
    units = slots // MB
    width = ends.shape[2]
    hidden_width = w_up.shape[2]
    slot_len = ends.shape[1] // slots
    mem_rows = slot_len // 8
    local = ends[0].reshape(slots, slot_len, width)
    wide_all = seg_group == 1

    def pick(table, batch):
        return lax.dynamic_slice_in_dim(table, batch * units, units, 0)

    def forward_run(operands):
        frames_in, memory_in, length, wide = operands
        return layer_forward(weights, frames_in, memory_in, length, wide, first)

    def forward_skip(operands):
        return forward_blank(units, slot_len, width, hidden_width)

    received_rows = jnp.zeros((units, slot_len, width), jnp.bfloat16)
    received_memory = jnp.zeros((units, mem_rows, width), jnp.bfloat16)
    kept_steps = []
    finals = []
    for step in range(MB + 1):
        batch = step - section
        running = (batch >= 0) & (batch < MB)
        batch = jnp.clip(batch, 0, MB - 1)
        frames_in = jnp.where(first, pick(local, batch), received_rows)
        operands = (frames_in, received_memory, pick(lengths, batch), pick(wide_all, batch))
        final, memory_out, kept = lax.cond(running, forward_run, forward_skip, operands)
        kept_steps.append(kept)
        finals.append(final)
        if step < MB:
            received_rows, received_memory = shifted((final, memory_out), "section", 1)
    kept_stack = jax.tree.map(lambda *items: jnp.stack(items), *kept_steps)

    def ffn_run(operands):
        kept, grad_final, length = operands
        return ffn_backward(weights, kept, grad_final, length)

    def attention_run(operands):
        kept, grad_after, grad_memory, length, wide = operands
        return attention_backward(weights, kept, grad_after, grad_memory, length, wide, first)

    def ffn_skip(operands):
        return ffn_blank(units, slot_len, width, hidden_width)

    def attention_skip(operands):
        return attention_blank(units, slot_len, width)

    received_grad = jnp.zeros((units, slot_len, width), jnp.bfloat16)
    received_grad_memory = jnp.zeros((units, mem_rows, width), jnp.bfloat16)
    totals_ffn = ffn_blank(units, slot_len, width, hidden_width)[1]
    totals_attention = attention_blank(units, slot_len, width)[2]
    grads_in = []
    summed_ffn = totals_ffn
    for step in range(MB + 1):
        batch = step - 1 + section
        running = (batch >= 0) & (batch < MB)
        batch = jnp.clip(batch, 0, MB - 1)
        position = batch + section
        kept = jax.tree.map(
            lambda stacked: lax.dynamic_index_in_dim(stacked, position, 0, keepdims=False),
            kept_stack,
        )
        length = pick(lengths, batch)
        wide = pick(wide_all, batch)
        grad_final = jnp.where(first, received_grad, pick(local, batch))
        grad_memory = jnp.where(first, received_grad_memory, jnp.zeros_like(received_grad_memory))
        grad_after, ffn_terms = lax.cond(running, ffn_run, ffn_skip, (kept, grad_final, length))
        totals_ffn = jax.tree.map(lambda total, term: total + term, totals_ffn, ffn_terms)
        if step == MB:
            summed_ffn = totals_ffn
        grad_inputs, grad_memory_in, attention_terms = lax.cond(
            running, attention_run, attention_skip, (kept, grad_after, grad_memory, length, wide)
        )
        totals_attention = jax.tree.map(
            lambda total, term: total + term, totals_attention, attention_terms
        )
        grads_in.append(grad_inputs)
        if step < MB:
            received_grad, received_grad_memory = shifted(
                (grad_inputs.astype(jnp.bfloat16), grad_memory_in.astype(jnp.bfloat16)),
                "section",
                -1,
            )
    summed_all = lax.psum(
        (
            totals_attention[0],
            totals_attention[1],
            totals_attention[2],
            totals_attention[3],
            totals_attention[4],
            totals_attention[5],
            totals_attention[6],
            totals_attention[7],
            summed_ffn[0],
            summed_ffn[1],
            summed_ffn[2],
            summed_ffn[3],
            summed_ffn[4],
            summed_ffn[5],
        ),
        "dp",
    )
    summed_attention = summed_all[:8]
    summed_ffn = summed_all[8:]
    input_grad = jnp.concatenate(grads_in[1:], axis=0).reshape(-1, width).astype(jnp.bfloat16)
    final_rows = jnp.concatenate(finals[1:], axis=0).reshape(-1, width)
    ends_out = jnp.where(first, input_grad, final_rows)[None]
    grad_gain = jnp.concatenate([summed_attention[0], summed_ffn[0]], axis=0)
    grad_shift = jnp.concatenate([summed_attention[1], summed_ffn[1]], axis=0)
    return (
        ends_out,
        grad_gain[None],
        grad_shift[None],
        summed_attention[2][None],
        summed_attention[3][None],
        summed_attention[4][None],
        summed_attention[5][None],
        summed_attention[6][None],
        summed_attention[7][None],
        summed_ffn[2][None],
        summed_ffn[3][None],
        summed_ffn[4][None],
        summed_ffn[5][None],
    )


def solution(mesh):
    placed = (
        P("section", "dp", None),
        P("dp"),
        P("dp"),
        P("section", None, None),
        P("section", None, None),
        P("section", None, None),
        P("section", None, None),
        P("section", None, None),
        P("section", None, None),
        P("section", None, None),
        P("section", None),
        P("section", None, None),
        P("section", None),
        P("section", None, None),
        P("section", None),
    )
    return jax.shard_map(
        on_device,
        mesh=mesh,
        in_specs=placed,
        out_specs=(
            P("section", "dp", None),
            P("section", None, None),
            P("section", None, None),
            P("section", None, None),
            P("section", None, None),
            P("section", None, None),
            P("section", None, None),
            P("section", None, None),
            P("section", None),
            P("section", None, None),
            P("section", None),
            P("section", None, None),
            P("section", None),
        ),
        check_vma=False,
    )
```

profile of v0, /device:TPU:0, one launch (start us, length us, event | category | flops | bytes accessed | tf_op | source)
XLA Modules:
  0.0 1568.0 jit_solution(15819234981330834677)
XLA Ops:
  9.6 121.9 %conditional.9 = (bf16[1,512,512]{1,2,0:T(8,128)(2,1)}, bf16[1,64,512]{2,1,0:T(8,128)(2,1)}, f32[1,1,1,4,8,144]{5,4,3,2,1,0:T(8,128)}, bf16[1,1,512,512]{3,2,1,0...) conditional(s32[]{:T(128)} %convert_element_type.1105, ...), branch_computations={%region_0.1_spmd, %region_1.20_spmd} | conditional | flops 3727842304 | bytes 127267296 | solution.py:616
  31.0 4.1 and_reduce_fusion
  35.6 4.0 and_reduce_fusion.2
  112.8 12.7 fusion.101
  164.6 194.1 %conditional.10 = (bf16[1,512,512]{1,2,0:T(8,128)(2,1)}, bf16[1,64,512]{2,1,0:T(8,128)(2,1)}, f32[1,1,1,4,8,144]{5,4,3,2,1,0:T(8,128)}, bf16[1,1,512,512]{3,2,1,...) conditional(s32[]{:T(128)} %convert_element_type.1106, ...), branch_computations={%region_18.21_spmd, %region_19.38_spmd} | conditional | flops 3727842304 | bytes 131404280 | solution.py:616
  186.2 4.0 and_reduce_fusion.4
  190.8 4.1 and_reduce_fusion.6
  335.7 13.4 fusion.189
  390.4 21.4 %conditional.11 = (f32[1,1,1,4,8,144]{5,4,3,2,1,0:T(8,128)}, bf16[1,1,512,512]{3,2,1,0:T(8,128)(2,1)S(1)}, bf16[1,1,512,2048]{3,2,1,0:T(8,128)(2,1)}, bf16[1,1,5...) conditional(s32[]{:T(128)} %convert_element_type.1107, ...), branch_computations={%region_36.39_spmd, %region_37.56_spmd} | conditional | flops 3694189568 | bytes 130681320 | solution.py:616
  446.1 13.2 conditional.13
  461.9 365.0 %collective-permute-done.4 = bf16[1,512,512]{2,1,0:T(8,128)(2,1)S(1)} collective-permute-done((bf16[1,512,512]{2,1,0:T(8,128)(2,1)}, bf16[1,512,512]{2,1,0:T(8,128)(2,1)S(1)}, u32[]{:S(2)}, u32[]{:S(2)}) %collective-permute-start.4) | collective-permute-done | bytes 524320 | tf_op jit(solution)/shard_map/ppermute | solution.py:19
  827.7 34.6 %conditional.14 = (f32[1,512,512]{2,1,0:T(8,128)}, f32[2,512]{1,0:T(2,128)S(1)}, f32[2,512]{1,0:T(2,128)S(1)}, f32[512,2048]{1,0:T(8,128)S(1)}, f32[2048]{0:T(10...) conditional(s32[]{:T(128)} %convert_element_type.1104, () %tuple.407, (bf16[2,512,512]{2,1,0:T(8,128)(2,1)}, ...), branch_computations={%region_92.95_spmd, %region_93.110_spmd} | conditional | flops 5460465152 | bytes 70176432 | solution.py:656
  842.0 12.3 convert_reduce_fusion.2
  865.6 188.6 %conditional.15 = (bf16[1,64,512]{2,1,0:T(8,128)(2,1)S(1)}, f32[1,512]{1,0:T(1,128)}, f32[1,512]{1,0:T(1,128)}, f32[512,512]{1,0:T(8,128)}, f32[512,512]{1,0:T(8...) conditional(s32[]{:T(128)} %convert_element_type.1104, ...), branch_computations={%region_108.111_spmd, %region_109.132_spmd} | conditional | flops 3137772288 | bytes 205138480 | solution.py:660
  900.8 3.9 and_reduce_fusion.22
  974.6 6.1 multiply_reduce_fusion.22
  1056.8 13.8 collective-permute-done.6
  1070.6 34.6 %conditional.16 = (f32[1,512,512]{2,1,0:T(8,128)}, f32[2,512]{1,0:T(2,128)S(1)}, f32[2,512]{1,0:T(2,128)S(1)}, f32[512,2048]{1,0:T(8,128)S(1)}, f32[2048]{0:T(10...) conditional(s32[]{:T(128)} %convert_element_type.1111, () %tuple.415, (bf16[2,512,512]{2,1,0:T(8,128)(2,1)}, ...), branch_computations={%region_130.133_spmd, %region_131.148_spmd} | conditional | flops 5460465152 | bytes 70176432 | solution.py:656
  1084.8 12.0 convert_reduce_fusion.4
  1108.6 177.9 %conditional.17 = (f32[1,512]{1,0:T(1,128)S(1)}, f32[1,512]{1,0:T(1,128)S(1)}, f32[512,512]{1,0:T(8,128)}, f32[512,512]{1,0:T(8,128)}, f32[512,512]{1,0:T(8,128)...) conditional(s32[]{:T(128)} %convert_element_type.1111, ...), branch_computations={%region_146.149_spmd, %region_147.170_spmd} | conditional | flops 3137772544 | bytes 200845920 | solution.py:660
  1212.2 6.0 multiply_reduce_fusion.23
  1286.6 8.6 add_bitcast_fusion.15
  1316.0 61.3 %all-reduce.54 = (f32[2,512]{1,0:T(2,128)S(1)}, f32[1,512]{1,0:T(1,128)S(1)}, f32[2,512]{1,0:T(2,128)S(1)}, f32[1,512]{1,0:T(1,128)S(1)}, f32[1,2,512]{2,1,0:T(2...) all-reduce(f32[2,512]{1,0:T(2,128)S(1)} %add_add_fusion.17, ...), channel_id=1, replica_groups=mesh['section'=2,'dp'=16] {'dp'}, use_global_device_ids=true, to_apply=%region_169.172 | all-reduce | flops 7168 | bytes 57344 | tf_op jit(solution)/shard_map/psum | solution.py:673
  1381.1 167.3 %all-reduce.58.cloned.1.call-done = (f32[1,512,512]{2,1,0:T(8,128)}, f32[1,512,512]{2,1,0:T(8,128)}, f32[1,512,512]{2,1,0:T(8,128)}, f32[1,512,512]{2,1,0:T(8,12...) async-done(((f32[1,512,512]{2,1,0:T(8,128)}, f32[1,512,512]{2,1,0:T(8,128)}, f32[1,512,512]{2,1,0:T(8,128)}, f32[1,512,512]{2,1,0:T(8,128)}, ...) | async-done | bytes 12582928 | tf_op jit(solution)/shard_map/psum | solution.py:673
  (1200 shorter events, 783.3 us)
Async XLA Ops:
  7.2 1541.2 %all-reduce.58.cloned.1.call-start = ((), (), s32[]{:S(2)}) async-start(), calls=%async_computation | async-start | bytes 25165824 | tf_op jit(solution)/shard_map/psum | solution.py:673
  89.8 18.2 %copy-start.1 = (bf16[512,512]{1,0:T(8,128)(2,1)S(1)}, bf16[512,512]{1,0:T(8,128)(2,1)}, u32[]{:S(2)}) copy-start(bf16[512,512]{1,0:T(8,128)(2,1)} %get-tuple-element.2006) | copy-start | bytes 1572868 | tf_op jit(solution)/shard_map/cond
  89.8 18.2 %copy-start.220 = (f32[1,512]{1,0:T(1,128)S(1)}, f32[1,512]{1,0:T(1,128)}, u32[]{:S(2)}) copy-start(f32[1,512]{1,0:T(1,128)} %get-tuple-element.2007) | copy-start | bytes 6148 | tf_op jit(solution)/shard_map/cond
  132.4 32.2 %collective-permute-start.1 = (bf16[1,64,512]{1,2,0:T(8,128)(2,1)S(1)}, bf16[1,64,512]{1,2,0:T(8,128)(2,1)}, u32[]{:S(2)}, u32[]{:S(2)}) collective-permute-start(bf16[1,64,512]{1,2,0:T(8,128)(2,1)S(1)} %copy.449), channel_id=1, source_target_pairs={{0,16},{1,17},{2,18},{3,19},{4,20},{5,21},{6,22},{7,23},{8,24},{9,... | collective-permute-start | bytes 196616 | tf_op jit(solution)/shard_map/ppermute | solution.py:19
  134.4 30.2 %collective-permute-start = (bf16[1,512,512]{1,2,0:T(8,128)(2,1)}, bf16[1,512,512]{1,2,0:T(8,128)(2,1)}, u32[]{:S(2)}, u32[]{:S(2)}) collective-permute-start(bf16[1,512,512]{1,2,0:T(8,128)(2,1)} %get-tuple-element.2281), channel_id=1, source_target_pairs={{0,16},{1,17},{2,18},{3,19},{4,20},{5,21},{6,22},{7,23},{8,24},{9,... | collective-permute-start | bytes 1572872 | tf_op jit(solution)/shard_map/ppermute | solution.py:19
  170.5 46.9 %copy-start.232 = (f32[512]{0:T(512)}, f32[512]{0:T(512)S(1)}, u32[]{:S(2)}) copy-start(f32[512]{0:T(512)S(1)} %fusion.258) | copy-start | bytes 6148 | tf_op jit(solution)/shard_map/cond
  271.0 19.4 %copy-start.87 = (pred[4,144,224]{2,1,0:T(8,128)(4,1)S(1)}, pred[4,144,224]{2,1,0:T(8,128)(4,1)}, u32[]{:S(2)}) copy-start(pred[4,144,224]{2,1,0:T(8,128)(4,1)} %add_bitcast_fusion.3) | copy-start | bytes 387076 | tf_op jit(solution)/shard_map/cond
  298.6 27.3 %copy-start.221 = (f32[1,512]{1,0:T(1,128)S(1)}, f32[1,512]{1,0:T(1,128)}, u32[]{:S(2)}) copy-start(f32[1,512]{1,0:T(1,128)} %get-tuple-element.2027) | copy-start | bytes 6148 | tf_op jit(solution)/shard_map/cond
  359.7 30.7 %collective-permute-start.3 = (bf16[1,64,512]{1,2,0:T(8,128)(2,1)S(1)}, bf16[1,64,512]{1,2,0:T(8,128)(2,1)}, u32[]{:S(2)}, u32[]{:S(2)}) collective-permute-start(bf16[1,64,512]{1,2,0:T(8,128)(2,1)S(1)} %copy.452), channel_id=1, source_target_pairs={{0,16},{1,17},{2,18},{3,19},{4,20},{5,21},{6,22},{7,23},{8,24},{9,... | collective-permute-start | bytes 196616 | tf_op jit(solution)/shard_map/ppermute | solution.py:19
  361.6 28.7 %collective-permute-start.2 = (bf16[1,512,512]{1,2,0:T(8,128)(2,1)}, bf16[1,512,512]{1,2,0:T(8,128)(2,1)}, u32[]{:S(2)}, u32[]{:S(2)}) collective-permute-start(bf16[1,512,512]{1,2,0:T(8,128)(2,1)} %get-tuple-element.2284), channel_id=1, source_target_pairs={{0,16},{1,17},{2,18},{3,19},{4,20},{5,21},{6,22},{7,23},{8,24},{9,... | collective-permute-start | bytes 1572872 | tf_op jit(solution)/shard_map/ppermute | solution.py:19
  459.2 367.6 %collective-permute-start.4 = (bf16[1,512,512]{2,1,0:T(8,128)(2,1)}, bf16[1,512,512]{2,1,0:T(8,128)(2,1)S(1)}, u32[]{:S(2)}, u32[]{:S(2)}) collective-permute-start(bf16[1,512,512]{2,1,0:T(8,128)(2,1)} %get-tuple-element.2330), channel_id=1, source_target_pairs={{16,0},{17,1},{18,2},{19,3},{20,4},{21,5},{22,6},{23,7},{24,8},{25... | collective-permute-start | bytes 1572872 | tf_op jit(solution)/shard_map/ppermute | solution.py:19
  460.6 401.8 %collective-permute-start.5 = (bf16[1,64,512]{2,1,0:T(8,128)(2,1)}, bf16[1,64,512]{2,1,0:T(8,128)(2,1)S(1)}, u32[]{:S(2)}, u32[]{:S(2)}) collective-permute-start(bf16[1,64,512]{2,1,0:T(8,128)(2,1)} %copy-done.219), channel_id=1, source_target_pairs={{16,0},{17,1},{18,2},{19,3},{20,4},{21,5},{22,6},{23,7},{24,8},{25... | collective-permute-start | bytes 196616 | tf_op jit(solution)/shard_map/ppermute | solution.py:19
  827.7 35.4 %copy-start.5 = (bf16[3,1,512,512]{3,2,1,0:T(8,128)(2,1)S(1)}, bf16[3,1,512,512]{3,2,1,0:T(8,128)(2,1)}, u32[]{:S(2)}) copy-start(bf16[3,1,512,512]{3,2,1,0:T(8,128)(2,1)} %copy-done.4) | copy-start | bytes 4718596
  827.7 35.4 %copy-start.31 = (bf16[3,1,64,512]{2,3,1,0:T(8,128)(2,1)S(1)}, bf16[3,1,64,512]{2,3,1,0:T(8,128)(2,1)}, u32[]{:S(2)}) copy-start(bf16[3,1,64,512]{2,3,1,0:T(8,128)(2,1)} %constant_dynamic-update-slice_fusion.3) | copy-start | bytes 589828
  827.7 35.4 %copy-start.308 = (pred[2]{0:T(512)(128)(4,1)S(1)}, pred[2]{0:T(512)(128)(4,1)}, u32[]{:S(2)}) copy-start(pred[2]{0:T(512)(128)(4,1)} %copy-done.306) | copy-start | bytes 10
  865.6 42.9 %copy-start.216 = (bf16[1,64,512]{2,1,0:T(8,128)(2,1)}, bf16[1,64,512]{2,1,0:T(8,128)(2,1)S(1)}, u32[]{:S(2)}) copy-start(bf16[1,64,512]{2,1,0:T(8,128)(2,1)S(1)} %get-tuple-element.2114) | copy-start | bytes 196612 | tf_op jit(solution)/shard_map/cond
  917.0 20.0 %copy-start.91 = (pred[4,144,224]{2,1,0:T(8,128)(4,1)}, pred[4,144,224]{2,1,0:T(8,128)(4,1)S(1)}, u32[]{:S(2)}) copy-start(pred[4,144,224]{2,1,0:T(8,128)(4,1)S(1)} %add_bitcast_fusion.11) | copy-start | bytes 387076 | tf_op jit(solution)/shard_map/cond
  1054.2 16.4 %copy-start.69 = (bf16[1,512,512]{2,1,0:T(8,128)(2,1)}, bf16[1,512,512]{2,1,0:T(8,128)(2,1)S(1)}, u32[]{:S(2)}) copy-start(bf16[1,512,512]{2,1,0:T(8,128)(2,1)S(1)} %get-tuple-element.2380) | copy-start | bytes 1572868
  1054.2 16.4 %collective-permute-start.6 = (bf16[1,512,512]{2,1,0:T(8,128)(2,1)S(1)}, bf16[1,512,512]{2,1,0:T(8,128)(2,1)}, u32[]{:S(2)}, u32[]{:S(2)}) collective-permute-start(bf16[1,512,512]{2,1,0:T(8,128)(2,1)S(1)} %get-tuple-element.2380), channel_id=1, source_target_pairs={{16,0},{17,1},{18,2},{19,3},{20,4},{21,5},{22,6},{23,7},{24,8},{25... | collective-permute-start | bytes 1572872 | tf_op jit(solution)/shard_map/ppermute | solution.py:19
  1055.5 49.8 %collective-permute-start.7 = (bf16[1,64,512]{2,1,0:T(8,128)(2,1)}, bf16[1,64,512]{2,1,0:T(8,128)(2,1)S(1)}, u32[]{:S(2)}, u32[]{:S(2)}) collective-permute-start(bf16[1,64,512]{2,1,0:T(8,128)(2,1)} %copy-done.218), channel_id=1, source_target_pairs={{16,0},{17,1},{18,2},{19,3},{20,4},{21,5},{22,6},{23,7},{24,8},{25... | collective-permute-start | bytes 196616 | tf_op jit(solution)/shard_map/ppermute | solution.py:19
  1070.6 34.7 %copy-start.32 = (bf16[3,1,64,512]{2,3,1,0:T(8,128)(2,1)S(1)}, bf16[3,1,64,512]{2,3,1,0:T(8,128)(2,1)}, u32[]{:S(2)}) copy-start(bf16[3,1,64,512]{2,3,1,0:T(8,128)(2,1)} %constant_dynamic-update-slice_fusion.3) | copy-start | bytes 589828
  1070.6 34.7 %copy-start.113 = (pred[1,64,512]{2,1,0:T(8,128)(4,1)S(1)}, pred[1,64,512]{2,1,0:T(8,128)(4,1)}, u32[]{:S(2)}) copy-start(pred[1,64,512]{2,1,0:T(8,128)(4,1)} %select_n.1439) | copy-start | bytes 98308
  1070.6 34.7 %copy-start.309 = (pred[2]{0:T(512)(128)(4,1)S(1)}, pred[2]{0:T(512)(128)(4,1)}, u32[]{:S(2)}) copy-start(pred[2]{0:T(512)(128)(4,1)} %copy-done.306) | copy-start | bytes 10
  1312.5 66.1 %copy-start.70 = (bf16[1,512,512]{2,1,0:T(8,128)(2,1)S(1)}, bf16[1,512,512]{2,1,0:T(8,128)(2,1)}, u32[]{:S(2)}) copy-start(bf16[1,512,512]{2,1,0:T(8,128)(2,1)} %copy-done.69) | copy-start | bytes 1572868
  (213 other events, 1013.1 us)
Sparse Core Ops, SparseCore 0:
  1312.7 235.6 all-reduce.57
where the time goes:
time: 1580 us; the launch traced here: 1570 us
  waiting for transfers between devices  546 us (35%)
  local copies, waits for them, and re-layouts  417 us (26%)
  other arithmetic  279 us (18%)
  matrix products  164 us (10%)
  loops' own time  72.4 us (5%)
  blocking collectives  61.3 us (4%)
    ppermute x8, waiting for transfers between devices, shifted(): return lax.ppermute(block, axis, route)  379 us
    psum x1, waiting for transfers between devices, on_device(): lax.psum((totals_attention[0], totals_attention[1], totals_attention[2],...  167 us
    another operation x38, other arithmetic  88.8 us
    unnamed x173, local copies, waits for them, and re-layouts  81.6 us
    psum x1, blocking collectives, on_device(): lax.psum((totals_attention[0], totals_attention[1], totals_attention[2],...  61.3 us
    cond x354, local copies, waits for them, and re-layouts  53.9 us
    another operation x30, local copies, waits for them, and re-layouts, on_device(): kept_stack = jax.tree.map(lambda *items: jnp.stack(items), *kept_steps)  39.3 us
    another operation x3, loops' own time, on_device(): lax.cond(running, forward_run, forward_skip, operands)  37.2 us
  transfers between devices with their start and end apart: 9, of which 3 were waited for; matrix products, arithmetic and copies ran while one was open for 8% of the time, Pallas kernels for 0%

commit v1 on v0

v1 whole, which is shorter than its diff:
```python
import functools
import jax
import jax.numpy as jnp
from jax import lax
from jax.experimental import pallas as pl
from jax.experimental.pallas import tpu as pltpu
from jax.sharding import PartitionSpec as P

LEFT = 30
RIGHT = 4
MEM = 4
TILE = 64
KEYS = 128
ROWS = 80
FRONT = 32
BF = jnp.bfloat16
F32 = jnp.float32
VMEM_LIMIT = 56 * 1024 * 1024


def dot(a, b):
    return lax.dot_general(a, b, (((1,), (0,)), ((), ())), preferred_element_type=F32)


def dot_nt(a, b):
    return lax.dot_general(a, b, (((1,), (1,)), ((), ())), preferred_element_type=F32)


def dot_tn(a, b):
    return lax.dot_general(a, b, (((0,), (0,)), ((), ())), preferred_element_type=F32)


def normed(value):
    center = value - jnp.mean(value, axis=-1, keepdims=True)
    rs = lax.rsqrt(jnp.mean(center * center, axis=-1, keepdims=True) + 1e-05)
    return center * rs, rs


def norm_back(w, xhat, rs):
    return (w - jnp.mean(w, axis=-1, keepdims=True) - xhat * jnp.mean(w * xhat, axis=-1, keepdims=True)) * rs


def fold8(value):
    rows, width = value.shape
    return jnp.sum(value.reshape(rows // 8, 8, width), axis=0)


def gelu_parts(f):
    half = jnp.exp(f * f * -0.5)
    t = 1.0 / (1.0 + jnp.abs(f) * (0.3275911 * 0.7071067811865476))
    poly = t * (0.5 * 0.254829592 + t * (0.5 * -0.284496736 + t * (0.5 * 1.421413741 + t * (0.5 * -1.453152027 + t * (0.5 * 1.061405429)))))
    tail = poly * half
    phi = jnp.where(f >= 0, 1.0 - tail, tail)
    return f * phi, phi + f * half * 0.3989422804014327


def seg_sizes(wide):
    return jnp.where(wide, 16, 8).astype(jnp.int32), jnp.where(wide, 4, 8).astype(jnp.int32)


def pool_matrix(length, wide, slot):
    seg, per = seg_sizes(wide)
    rows = slot // 8
    e = lax.broadcasted_iota(jnp.int32, (rows, slot), 0)
    t = lax.broadcasted_iota(jnp.int32, (rows, slot), 1)
    r = jnp.bitwise_and(e, 7)
    start = jnp.right_shift(e, 3) * TILE + r * seg
    inside = (t >= start) & (t < start + seg) & (t < length) & (r < per)
    e1 = lax.broadcasted_iota(jnp.int32, (rows, 1), 0)
    r1 = jnp.bitwise_and(e1, 7)
    start1 = jnp.right_shift(e1, 3) * TILE + r1 * seg
    count = jnp.where(r1 < per, jnp.clip(length - start1, 0, seg), 0)
    inverse = 1.0 / jnp.maximum(count, 1).astype(F32)
    return jnp.where(inside, 1.0, 0.0).astype(BF), inverse


def unpool(matrix, value):
    high = value.astype(BF)
    low = (value - high.astype(F32)).astype(BF)
    return dot_tn(jnp.concatenate([matrix, matrix], axis=0), jnp.concatenate([high, low], axis=0))


def tile_bias(tile, odd, length, wide):
    seg, per = seg_sizes(wide)
    row = lax.broadcasted_iota(jnp.int32, (ROWS, 1), 0)
    col = lax.broadcasted_iota(jnp.int32, (1, KEYS), 1)
    anchor = tile * TILE
    is_frame = row < TILE
    extra = row - TILE
    shift = jnp.where(wide, 4, 3).astype(jnp.int32)
    r = jnp.where(is_frame, jnp.right_shift(row, shift), jnp.bitwise_and(extra, 7))
    owned = is_frame | ((jnp.right_shift(extra, 3) == odd) & (r < per))
    key = col - (16 + FRONT)
    low = jnp.where(owned, r * seg - LEFT, 100000)
    high = jnp.minimum(r * seg + seg + RIGHT, length - anchor)
    frame_ok = (key >= jnp.maximum(low, -anchor)) & (key < high) & (col >= 16)
    c = jnp.bitwise_and(col, 7)
    slot = jnp.where((col < 16) & (c < per), jnp.where(col < 8, c - per, c), -100000)
    slot = jnp.where((col < 8) & (anchor == 0), -100000, slot)
    mem_ok = (slot >= r - MEM) & (slot < jnp.where(is_frame, r, -100000))
    return jnp.where(frame_ok | mem_ok, 0.0, -1e30).astype(F32)


def head_masks(rows):
    lane = jnp.right_shift(lax.broadcasted_iota(jnp.int32, (rows, 256), 1), 6)
    return [lane == h for h in range(4)]


def spread_heads(tile, masks):
    zero = jnp.zeros_like(tile)
    return jnp.concatenate([jnp.where(m, tile, zero) for m in masks], axis=0)


def gather_heads(stack, masks):
    total = jnp.where(masks[0], stack[:ROWS], 0.0)
    for h in range(1, 4):
        total = jnp.where(masks[h], stack[h * ROWS : (h + 1) * ROWS], total)
    return total


def key_window(pair, odd, lanes, frames_ref, even_ref, pad_ref):
    first = pl.multiple_of(pair * 16, 16)
    memory = even_ref[pl.ds(first, 16), lanes] if odd else pad_ref[pl.ds(first, 16), lanes]
    start = pl.multiple_of(pair * 128 + odd * 64, 64)
    return jnp.concatenate([memory, frames_ref[pl.ds(start, KEYS - 16), lanes]], axis=0)


def fill_windows(all_rows, frames_ref, even_ref, pad_ref, mem_rows, slot):
    width = all_rows.shape[1]
    memory = all_rows[:mem_rows].astype(F32)
    blank = jnp.zeros((8, width), F32)
    even_ref[...] = memory.astype(BF)
    pad_ref[...] = jnp.concatenate([blank, memory, blank], axis=0).astype(BF)
    frames_ref[:FRONT] = jnp.zeros((FRONT, width), BF)
    frames_ref[FRONT : FRONT + slot] = all_rows[mem_rows:].astype(BF)
    frames_ref[FRONT + slot :] = jnp.zeros((16, width), BF)


def attention_in(utt, lower, slot, pos_ref, len_ref, grp_ref, x_ref, mem_ref, gain, shift, wq, wk, wv, qvb, wo, ob,
                 *refs):
    (uc, mem, q, k, v, prob, mix, xh0, xh1, h, rs, after, memnext, kf, ke, kp, vf, ve, vp) = refs[-19:]
    mem_rows = slot // 8
    length = len_ref[utt]
    wide = grp_ref[utt] == 1
    g0, s0 = gain[0:1], shift[0:1]
    lane = lax.broadcasted_iota(jnp.int32, (1, 128), 1)

    def rows_in(i, carry):
        r = pl.ds(pl.multiple_of(i * 32, 32), 32)
        xhat, scale = normed(x_ref[r].astype(F32))
        xh0[0, r] = xhat.astype(BF)
        uc[0, r] = (xhat * g0 + s0).astype(BF)
        rs[0, r] = jnp.broadcast_to(scale, (32, 128))
        return carry

    lax.fori_loop(0, slot // 32, rows_in, 0, unroll=2)
    pm, inverse = pool_matrix(length, wide, slot)
    uc[0, slot:] = (dot(pm, uc[0, :slot]) * inverse).astype(BF)
    if lower:
        mem[0] = (dot(pm, x_ref[...]) * inverse).astype(BF)
    else:
        mem[0] = mem_ref[...]
    q[0] = (dot(uc[0], wq[...]) + qvb[0:1]).astype(BF)
    k[0, :mem_rows] = dot(mem[0], wk[...]).astype(BF)
    k[0, mem_rows:] = dot(uc[0, :slot], wk[...]).astype(BF)
    v[0, :mem_rows] = (dot(mem[0], wv[...]) + qvb[1:2]).astype(BF)
    v[0, mem_rows:] = (dot(uc[0, :slot], wv[...]) + qvb[1:2]).astype(BF)
    fill_windows(k[0], kf, ke, kp, mem_rows, slot)
    fill_windows(v[0], vf, ve, vp, mem_rows, slot)
    masks = head_masks(ROWS)

    def pair_step(pair, carry):
        for quad in range(2):
            lanes = slice(quad * 256, quad * 256 + 256)
            extra = None
            for odd in range(2):
                rows = pl.ds(pl.multiple_of(pair * 128 + odd * 64, 64), 64)
                srows = pl.ds(pl.multiple_of(slot + pair * 16, 16), 16)
                bias = tile_bias(pair * 2 + odd, odd, length, wide)
                qs = spread_heads(jnp.concatenate([q[0, rows, lanes], q[0, srows, lanes]], axis=0), masks)
                kw = key_window(pair, odd, lanes, kf, ke, kp)
                vw = key_window(pair, odd, lanes, vf, ve, vp)
                s = dot_nt(qs, kw).reshape(4, ROWS, KEYS) * 0.125 + bias[None]
                peak = jnp.maximum(jnp.max(s, axis=-1, keepdims=True), -1e29)
                e = jnp.exp(s - peak)
                total = jnp.sum(e, axis=-1, keepdims=True)
                p = (e * (1.0 / jnp.maximum(total, 1e-30))).astype(BF).reshape(4 * ROWS, KEYS)
                prob[0, pair * 4 + quad * 2 + odd] = p
                o = gather_heads(dot(p, vw), masks)
                mix[0, rows, lanes] = o[:TILE].astype(BF)
                extra = o[TILE:] if extra is None else extra + o[TILE:]
            mix[0, srows, lanes] = extra.astype(BF)
        return carry

    lax.fori_loop(0, slot // 128, pair_step, 0)
    z = dot(mix[0], wo[...]) + ob[...]
    memnext[...] = z[slot:].astype(BF)
    after[...] = z[:slot]
    g1, s1 = gain[1:2], shift[1:2]

    def rows_out(i, carry):
        r = pl.ds(pl.multiple_of(i * 32, 32), 32)
        a = x_ref[r].astype(F32) + after[r]
        after[r] = a
        xhat, scale = normed(a)
        xh1[0, r] = xhat.astype(BF)
        h[0, r] = (xhat * g1 + s1).astype(BF)
        rs[0, r] = jnp.where(lane == 0, rs[0, r], jnp.broadcast_to(scale, (32, 128)))
        return carry

    lax.fori_loop(0, slot // 32, rows_out, 0, unroll=2)


def ffn_in(utt, block, pos_ref, len_ref, h, after, gain, shift, wu, ub, wd, db, *refs):
    g, gp, xh2, rs2, y = refs[-5:]
    width = after.shape[1]
    total = after[...] + db[...]
    hid = h[0]
    for c in range(wu.shape[1] // 512):
        cols = slice(c * 512, c * 512 + 512)
        act, slope = gelu_parts(dot(hid, wu[:, cols]) + ub[:, cols])
        act = act.astype(BF)
        g[0, :, cols] = act
        gp[0, :, cols] = slope.astype(BF)
        total = total + dot(act, wd[cols])
    xhat, scale = normed(total)
    xh2[0] = xhat.astype(BF)
    rs2[0] = jnp.broadcast_to(scale, (block, 128))
    t = lax.broadcasted_iota(jnp.int32, (block, 1), 0) + pl.program_id(0) * block
    valid = jnp.where(t < len_ref[utt], 1.0, 0.0)
    y[...] = ((xhat * gain[2:3] + shift[2:3]) * valid).astype(BF)


def ffn_back(utt, block, pos_ref, len_ref, cot, xh2, rs2, gp, xh1, rs, gain, wu, wd, *refs):
    gd, gf, gz, ga, small, acc = refs[-6:]
    step = pl.program_id(0)
    t = lax.broadcasted_iota(jnp.int32, (block, 1), 0) + step * block
    valid = jnp.where(t < len_ref[utt], 1.0, 0.0)

    @pl.when(step == 0)
    def _():
        acc[...] = jnp.zeros_like(acc)

    gv = cot[...].astype(F32) * valid
    xhat = xh2[0].astype(F32)
    acc[0] += fold8(gv * xhat)
    acc[1] += fold8(gv)
    ga2 = norm_back(gv * gain[2:3], xhat, rs2[0, :, 0:1])
    gdl = ga2.astype(BF)
    gd[0] = gdl
    acc[2] += fold8(gdl.astype(F32))
    back = None
    for c in range(wu.shape[1] // 512):
        cols = slice(c * 512, c * 512 + 512)
        gfl = (dot_nt(gdl, wd[cols]) * gp[0, :, cols].astype(F32)).astype(BF)
        gf[0, :, cols] = gfl
        acc[6 + c] += fold8(gfl.astype(F32))
        part = dot_nt(gfl, wu[:, cols])
        back = part if back is None else back + part
    xhat = xh1[0].astype(F32)
    acc[3] += fold8(back * xhat)
    acc[4] += fold8(back)
    total = ga2 + norm_back(back * gain[1:2], xhat, rs[0, :, 1:2])
    ga[...] = total
    gzl = total.astype(BF)
    gz[0] = gzl
    acc[5] += fold8(gzl.astype(F32))

    @pl.when(step == pl.num_programs(0) - 1)
    def _():
        small[...] = jnp.sum(acc[...], axis=1)


def attention_back(utt, lower, slot, pos_ref, len_ref, grp_ref, gz, gmem, ga, q, k, v, prob, xh0, rs, gain,
                   wq, wk, wv, wo, *refs):
    (gq, gk, gv, gzs, gx, gm, small, kf, ke, kp, vf, ve, vp, gof, gos, akf, akm, avf, avm, gu, acc) = refs[-21:]
    mem_rows = slot // 8
    width = gu.shape[1]
    length = len_ref[utt]
    wide = grp_ref[utt] == 1
    fill_windows(k[0], kf, ke, kp, mem_rows, slot)
    fill_windows(v[0], vf, ve, vp, mem_rows, slot)
    gof[...] = dot_nt(gz[0], wo[...]).astype(BF)
    if lower:
        gzs[0] = gmem[...]
        gos[...] = dot_nt(gmem[...], wo[...]).astype(BF)
    else:
        gzs[0] = jnp.zeros_like(gzs[0])
        gos[...] = jnp.zeros_like(gos)
    for ref in (akf, akm, avf, avm):
        ref[...] = jnp.zeros_like(ref)
    masks = head_masks(ROWS)

    def pair_step(pair, carry):
        for quad in range(2):
            lanes = slice(quad * 256, quad * 256 + 256)
            extra = None
            srows = pl.ds(pl.multiple_of(slot + pair * 16, 16), 16)
            for odd in range(2):
                rows = pl.ds(pl.multiple_of(pair * 128 + odd * 64, 64), 64)
                qs = spread_heads(jnp.concatenate([q[0, rows, lanes], q[0, srows, lanes]], axis=0), masks)
                gos_rows = gos[pl.ds(pl.multiple_of(pair * 16, 16), 16), lanes]
                go = spread_heads(jnp.concatenate([gof[rows, lanes], gos_rows], axis=0), masks)
                kw = key_window(pair, odd, lanes, kf, ke, kp)
                vw = key_window(pair, odd, lanes, vf, ve, vp)
                p = prob[0, pair * 4 + quad * 2 + odd]
                gprob = dot_nt(go, vw) * p.astype(F32)
                gs = (gprob - p.astype(F32) * jnp.sum(gprob, axis=-1, keepdims=True)).astype(BF)
                gqt = gather_heads(dot(gs, kw), masks) * 0.125
                gkt = dot_tn(gs, qs) * 0.125
                gvt = dot_tn(p, go)
                gq[0, rows, lanes] = gqt[:TILE].astype(BF)
                extra = gqt[TILE:] if extra is None else extra + gqt[TILE:]
                mrows = pl.ds(pl.multiple_of(pair * 16 + odd * 8, 8), 16)
                frows = pl.ds(pl.multiple_of(pair * 128 + odd * 64, 64), KEYS - 16)
                akm[mrows, lanes] += gkt[:16]
                akf[frows, lanes] += gkt[16:]
                avm[mrows, lanes] += gvt[:16]
                avf[frows, lanes] += gvt[16:]
            gq[0, srows, lanes] = extra.astype(BF)
        return carry

    lax.fori_loop(0, slot // 128, pair_step, 0)
    for out, am, af in ((gk, akm, akf), (gv, avm, avf)):
        out[0, :mem_rows] = am[8 : 8 + mem_rows].astype(BF)
        out[0, mem_rows:] = af[FRONT : FRONT + slot].astype(BF)
    pm, inverse = pool_matrix(length, wide, slot)
    gmf = dot_nt(gk[0, :mem_rows], wk[...]) + dot_nt(gv[0, :mem_rows], wv[...])
    gm[...] = gmf.astype(BF)
    gc = dot_nt(gq[0, slot:], wq[...]) * inverse
    gu[...] = (dot_nt(gk[0, mem_rows:], wk[...]) + dot_nt(gv[0, mem_rows:], wv[...])
               + dot_nt(gq[0, :slot], wq[...]) + unpool(pm, gc))
    acc[...] = jnp.zeros_like(acc)
    if lower:
        akf[:slot] = unpool(pm, gmf * inverse)
    g0 = gain[0:1]

    def rows_out(i, carry):
        r = pl.ds(pl.multiple_of(i * 32, 32), 32)
        w = gu[r]
        xhat = xh0[0, r].astype(F32)
        acc[0] += fold8(w * xhat)
        acc[1] += fold8(w)
        total = ga[r] + norm_back(w * g0, xhat, rs[0, r, 0:1])
        if lower:
            total = total + akf[r]
        gx[r] = total.astype(BF)
        return carry

    lax.fori_loop(0, slot // 32, rows_out, 0, unroll=2)
    acc[2] = fold8(gq[0].astype(F32))
    acc[3] = fold8(gv[0].astype(F32))
    acc[4] = fold8(gzs[0].astype(F32))
    small[...] = jnp.sum(acc[...], axis=1)


def full(shape):
    return pl.BlockSpec(shape, lambda *_: (0,) * len(shape))


def slotted(shape):
    return pl.BlockSpec((1,) + shape, lambda i, pos, *_: (pos[0],) + (0,) * len(shape))


def slotted_rows(shape):
    return pl.BlockSpec((1,) + shape, lambda i, pos, *_: (pos[0], i) + (0,) * (len(shape) - 1))


def rows_of(shape):
    return pl.BlockSpec(shape, lambda i, *_: (i,) + (0,) * (len(shape) - 1))


def sds(shape, dtype):
    return jax.ShapeDtypeStruct(shape, dtype)


def run(body, grid, scalars, inputs, kept, outs, scratch, cost):
    extra = list(kept) if kept is not None else []
    aliases = {len(scalars) + len(inputs) + i: i for i in range(len(extra))}
    return pl.pallas_call(
        body,
        grid_spec=pltpu.PrefetchScalarGridSpec(
            num_scalar_prefetch=len(scalars),
            grid=grid,
            in_specs=[spec for _, spec in inputs] + [pl.BlockSpec(memory_space=pl.ANY)] * len(extra),
            out_specs=[spec for _, spec in outs],
            scratch_shapes=scratch,
        ),
        out_shape=[shape for shape, _ in outs],
        input_output_aliases=aliases,
        compiler_params=pltpu.CompilerParams(vmem_limit_bytes=VMEM_LIMIT, dimension_semantics=("arbitrary",)),
        cost_estimate=cost,
    )(*scalars, *[a for a, _ in inputs], *extra)


def cost_of(flops, moved, special=0):
    return pl.CostEstimate(flops=int(flops), bytes_accessed=int(moved), transcendentals=int(special))


def window_scratch(slot, width):
    mem_rows = slot // 8
    one = [
        pltpu.VMEM((FRONT + slot + 16, width), BF),
        pltpu.VMEM((mem_rows, width), BF),
        pltpu.VMEM((mem_rows + 16, width), BF),
    ]
    return one + one


ROOMS = 3


def forward(weights, utt, lower, scalars, frames, memory, kept):
    (gain, shift, wq, wk, wv, qvb, wo, ob, wu, ub, wd, db) = weights
    slot, width = frames.shape
    hid = wu.shape[1]
    mem_rows = slot // 8
    every = slot + mem_rows
    pairs = slot // 128
    kept_a, kept_f = kept if kept is not None else (None, None)
    low = lambda *s: sds((ROOMS,) + s, BF)
    outs = [(low(*s), slotted(s)) for s in (
        (every, width), (mem_rows, width), (every, width), (every, width), (every, width),
        (pairs * 4, 4 * ROWS, KEYS), (every, width), (slot, width), (slot, width), (slot, width))]
    outs.append((sds((ROOMS, slot, 128), F32), slotted((slot, 128))))
    n_kept = len(outs)
    outs.append((sds((slot, width), F32), full((slot, width))))
    outs.append((sds((mem_rows, width), BF), full((mem_rows, width))))
    ins = [(a, full(a.shape)) for a in (frames, memory, gain, shift, wq, wk, wv, qvb, wo, ob)]
    res = run(
        functools.partial(attention_in, utt, lower, slot), (1,), scalars, ins, kept_a, outs,
        window_scratch(slot, width), cost_of(8 * every * width * width, 12 * every * width * 2, 8 * slot * 128))
    kept_a, (after, memnext) = res[:n_kept], res[n_kept:]
    h = kept_a[9]
    block = slot // 2
    ins = [(h, slotted_rows((block, width))), (after, rows_of((block, width)))]
    ins += [(a, full(a.shape)) for a in (gain, shift, wu, ub, wd, db)]
    outs = [(low(slot, hid), slotted_rows((block, hid))), (low(slot, hid), slotted_rows((block, hid))),
            (low(slot, width), slotted_rows((block, width))),
            (sds((ROOMS, slot, 128), F32), slotted_rows((block, 128))),
            (sds((slot, width), BF), rows_of((block, width)))]
    res = run(functools.partial(ffn_in, utt, block), (slot // block,), scalars[:2], ins, kept_f, outs, [],
              cost_of(4 * slot * width * hid, 4 * slot * hid + 4 * width * hid, slot * hid * 2))
    return res[4], memnext, (kept_a, res[:4])


def backward_ffn(weights, utt, scalars, cot, kept, grads):
    (gain, shift, wq, wk, wv, qvb, wo, ob, wu, ub, wd, db) = weights
    slot, width = cot.shape
    hid = wu.shape[1]
    block = slot // 2
    kept_a, kept_f = kept
    ins = [(cot, rows_of((block, width))), (kept_f[2], slotted_rows((block, width))),
           (kept_f[3], slotted_rows((block, 128))), (kept_f[1], slotted_rows((block, hid))),
           (kept_a[8], slotted_rows((block, width))), (kept_a[10], slotted_rows((block, 128)))]
    ins += [(a, full(a.shape)) for a in (gain, wu, wd)]
    low = lambda *s: sds((ROOMS,) + s, BF)
    outs = [(low(slot, width), slotted_rows((block, width))), (low(slot, hid), slotted_rows((block, hid))),
            (low(slot, width), slotted_rows((block, width))), (sds((slot, width), F32), rows_of((block, width))),
            (sds((16, width), F32), full((16, width)))]
    res = run(functools.partial(ffn_back, utt, block), (slot // block,), scalars[:2], ins, grads, outs,
              [pltpu.VMEM((16, 8, width), F32)],
              cost_of(4 * slot * width * hid, 4 * slot * hid + 4 * width * hid))
    return res[:3], res[3], res[4]


def backward_attention(weights, utt, lower, scalars, gz, gmem, ga, kept, grads):
    (gain, shift, wq, wk, wv, qvb, wo, ob, wu, ub, wd, db) = weights
    slot, width = ga.shape
    mem_rows = slot // 8
    every = slot + mem_rows
    (uc, mem, q, k, v, prob, mix, xh0, xh1, h, rs), _ = kept
    ins = [(gz, slotted((slot, width))), (gmem, full(gmem.shape)), (ga, full(ga.shape))]
    ins += [(a, slotted(a.shape[1:])) for a in (q, k, v, prob, xh0, rs)]
    ins += [(a, full(a.shape)) for a in (gain, wq, wk, wv, wo)]
    low = lambda *s: sds((ROOMS,) + s, BF)
    outs = [(low(*s), slotted(s)) for s in ((every, width),) * 3 + ((mem_rows, width),)]
    outs += [(sds((slot, width), BF), full((slot, width))), (sds((mem_rows, width), BF), full((mem_rows, width))),
             (sds((16, width), F32), full((16, width)))]
    scratch = window_scratch(slot, width) + [
        pltpu.VMEM((slot, width), BF), pltpu.VMEM((mem_rows, width), BF),
        pltpu.VMEM((FRONT + slot + 16, width), F32), pltpu.VMEM((mem_rows + 16, width), F32),
        pltpu.VMEM((FRONT + slot + 16, width), F32), pltpu.VMEM((mem_rows + 16, width), F32),
        pltpu.VMEM((slot, width), F32), pltpu.VMEM((16, 8, width), F32)]
    res = run(functools.partial(attention_back, utt, lower, slot), (1,), scalars, ins, grads, outs, scratch,
              cost_of(8 * every * width * width, 12 * every * width * 2))
    return res[:4], res[4], res[5], res[6]


def ffn_weights(g, gd, h, gf, out):
    step = pl.program_id(0)
    half = pl.num_programs(0) // 2

    @pl.when(step < half)
    def _():
        out[0] = sum(dot_tn(g[u], gd[u]) for u in range(g.shape[0])).astype(out.dtype)

    @pl.when(step >= half)
    def _():
        out[0] = sum(dot_tn(h[u], gf[u]) for u in range(h.shape[0])).astype(out.dtype)


def weight_grads_ffn(slots, g, gd, h, gf):
    _, slot, hid = g.shape
    width = gd.shape[2]
    blocks = hid // width
    spec = lambda index: pl.BlockSpec((slots, slot, width), index)
    return pl.pallas_call(
        ffn_weights,
        grid=(2 * blocks,),
        in_specs=[spec(lambda j: (0, 0, jnp.minimum(j, blocks - 1))), spec(lambda j: (0, 0, 0)),
                  spec(lambda j: (0, 0, 0)), spec(lambda j: (0, 0, jnp.maximum(j - blocks, 0)))],
        out_specs=pl.BlockSpec((1, width, width), lambda j: (j, 0, 0)),
        out_shape=sds((2 * blocks, width, width), BF),
        compiler_params=pltpu.CompilerParams(vmem_limit_bytes=VMEM_LIMIT, dimension_semantics=("arbitrary",)),
        cost_estimate=cost_of(4 * slots * slot * hid * width, 4 * slots * slot * hid + 4 * hid * width),
    )(g, gd, h, gf)


def attention_weights(uc, mem, mix, gq, gk, gv, gz, gzs, out):
    step = pl.program_id(0)
    slots, every, width = uc.shape
    slot = gz.shape[1]
    mem_rows = every - slot

    @pl.when(step == 0)
    def _():
        out[0] = sum(dot_tn(uc[u], gq[u]) for u in range(slots)).astype(out.dtype)

    for place, ref in ((1, gk), (2, gv)):
        @pl.when(step == place)
        def _():
            out[0] = sum(dot_tn(mem[u], ref[u, :mem_rows]) + dot_tn(uc[u, :slot], ref[u, mem_rows:])
                         for u in range(slots)).astype(out.dtype)

    @pl.when(step == 3)
    def _():
        out[0] = sum(dot_tn(mix[u, :slot], gz[u]) + dot_tn(mix[u, slot:], gzs[u])
                     for u in range(slots)).astype(out.dtype)


def weight_grads_attention(slots, *arrays):
    _, every, width = arrays[0].shape
    return pl.pallas_call(
        attention_weights,
        grid=(4,),
        in_specs=[pl.BlockSpec((slots,) + a.shape[1:], lambda j: (0, 0, 0)) for a in arrays],
        out_specs=pl.BlockSpec((1, width, width), lambda j: (j, 0, 0)),
        out_shape=sds((4, width, width), BF),
        compiler_params=pltpu.CompilerParams(vmem_limit_bytes=VMEM_LIMIT, dimension_semantics=("arbitrary",)),
        cost_estimate=cost_of(8 * slots * every * width * width, 16 * slots * every * width),
    )(*arrays)


def shifted(block, axis, distance):
    devices = range(lax.axis_size(axis))
    route = [(i - distance, i) for i in devices if i - distance in devices]
    return lax.ppermute(block, axis, route)


def on_device(ends, lengths, seg_group, norm_gain, norm_shift, w_query, w_key, w_value, qv_bias, w_out, out_bias,
              w_up, up_bias, w_down, down_bias):
    weights = (norm_gain[0], norm_shift[0], w_query[0], w_key[0], w_value[0], qv_bias[0], w_out[0], out_bias,
               w_up[0], up_bias, w_down[0], down_bias)
    section = lax.axis_index("section")
    first = section == 0
    slots = lengths.shape[0]
    width = ends.shape[2]
    slot = ends.shape[1] // slots
    mem_rows = slot // 8
    hid = w_up.shape[2]
    local = ends[0].reshape(slots, slot, width)
    lower = [(jnp.where(first, b, ROOMS - 1).astype(jnp.int32).reshape(1), lengths, seg_group) for b in range(slots)]
    upper = [(jnp.where(first, ROOMS - 1, b).astype(jnp.int32).reshape(1), lengths, seg_group) for b in range(slots)]
    blank = jnp.zeros((mem_rows, width), BF)

    kept = None
    sent = []
    for b in range(slots):
        y, memory, kept = forward(weights, b, True, lower[b], local[b], blank, kept)
        sent.append(shifted((y, memory), "section", 1))
    finals = []
    for b in range(slots):
        y, _, kept = forward(weights, b, False, upper[b], sent[b][0], sent[b][1], kept)
        finals.append(y)

    kept_a, kept_f = kept
    grads_f = grads_a = None
    smalls = [[], []]
    sent = []
    for b in range(slots):
        grads_f, ga, small_f = backward_ffn(weights, b, upper[b], local[b], kept, grads_f)
        grads_a, gx, gm, small_a = backward_attention(weights, b, False, upper[b], grads_f[2], blank, ga, kept, grads_a)
        smalls[1].append((small_f, small_a))
        sent.append(shifted((gx, gm), "section", -1))
    inputs_back = []
    held = []
    for b in range(slots):
        grads_f, ga, small_f = backward_ffn(weights, b, lower[b], sent[b][0], kept, grads_f)
        if b == slots - 1:
            wide_sums = weight_grads_ffn(slots, kept_f[0], grads_f[0], kept_a[9], grads_f[1])
            wide_sums = lax.psum(wide_sums, "dp")
        grads_a, gx, gm, small_a = backward_attention(weights, b, True, lower[b], grads_f[2], sent[b][1], ga, kept, grads_a)
        smalls[0].append((small_f, small_a))
        inputs_back.append(gx)
    square = weight_grads_attention(slots, kept_a[0], kept_a[1], kept_a[6], grads_a[0], grads_a[1], grads_a[2],
                                    grads_f[2], grads_a[3])
    square = lax.psum(square, "dp")

    def total(side, part):
        return sum(smalls[side][b][part] for b in range(slots))

    small_f = jnp.where(first, total(0, 0), total(1, 0))
    small_a = jnp.where(first, total(0, 1), total(1, 1))
    small = jnp.concatenate([
        jnp.stack([small_a[0], small_f[3], small_f[0], small_a[1], small_f[4], small_f[1], small_a[2], small_a[3],
                   small_f[5] + small_a[4], small_f[2]]), small_f[6 : 6 + hid // width]], axis=0)
    small = lax.psum(small, "dp")
    ends_out = jnp.where(first, jnp.stack(inputs_back), jnp.stack(finals)).reshape(1, slots * slot, width)
    blocks = hid // width
    down = wide_sums[:blocks].astype(F32).reshape(1, hid, width)
    up = jnp.transpose(wide_sums[blocks:].astype(F32), (1, 0, 2)).reshape(1, width, hid)
    square = square.astype(F32)
    return (ends_out, small[None, 0:3], small[None, 3:6], square[0:1], square[1:2], square[2:3], small[None, 6:8],
            square[3:4], small[8:9], up, small[10:].reshape(1, hid), down, small[9:10])


def solution(mesh):
    placed = (
        P("section", "dp", None), P("dp"), P("dp"),
        P("section", None, None), P("section", None, None), P("section", None, None), P("section", None, None),
        P("section", None, None), P("section", None, None), P("section", None, None), P("section", None),
        P("section", None, None), P("section", None), P("section", None, None), P("section", None),
    )
    return jax.shard_map(
        on_device,
        mesh=mesh,
        in_specs=placed,
        out_specs=(
            P("section", "dp", None), P("section", None, None), P("section", None, None), P("section", None, None),
            P("section", None, None), P("section", None, None), P("section", None, None), P("section", None, None),
            P("section", None), P("section", None, None), P("section", None), P("section", None, None),
            P("section", None),
        ),
        check_vma=False,
    )
```

time: 1580 us -> 443 us (0.28)
  waiting for transfers between devices: 546 us -> 87 us
  local copies, waits for them, and re-layouts: 417 us -> 26.3 us
  other arithmetic: 279 us -> 6.52 us
  Pallas kernels: 0 us -> 224 us
  matrix products: 164 us -> 0 us
  loops' own time: 72.4 us -> 0 us
    ppermute x8, waiting for transfers between devices: 379 us -> 12.2 us  [shifted(): return lax.ppermute(block, axis, route)]
    pallas_call x0 -> x18, Pallas kernels: none -> 224 us  [the longest x16 205 us: run(): pl.pallas_call(body, grid_spec=pltpu.PrefetchScalarGridSpec(num_scalar_pr...]
    dot_general x64 -> x0, matrix products: 164 us -> none  [the longest x2 26.1 us: layer_forward(): jnp.einsum('usd,df->usf', hidden_in, w_up, preferred_element_type=jnp.flo...]
    psum x1, waiting for transfers between devices: 167 us -> 74.7 us  [on_device(): square = lax.psum(square, 'dp')]
    another operation x48 -> x0, other arithmetic: 92.2 us -> none
    cond x381 -> x0, local copies, waits for them, and re-layouts: 89 us -> none
    another operation x9 -> x0, loops' own time: 72.4 us -> none  [the longest x3 37.2 us: on_device(): lax.cond(running, forward_run, forward_skip, operands)]
    another operation x82 -> x0, local copies, waits for them, and re-layouts: 70.3 us -> none  [the longest x30 39.3 us: on_device(): kept_stack = jax.tree.map(lambda *items: jnp.stack(items), *kept_steps)]
  transfers between devices with their start and end apart: 9 -> 9, of which waited for: 3 -> 3; matrix products, arithmetic and copies ran while one was open for 8% -> 1% of each run, Pallas kernels for 0% -> 28%
where the time goes in v1:
time: 443 us; the launch traced here: 434 us
  Pallas kernels  224 us (51%)
  waiting for transfers between devices  87 us (20%)
  blocking collectives  61.1 us (14%)
  local copies, waits for them, and re-layouts  26.3 us (6%)
  between operations  14.9 us (3%)
  starting transfers between devices  14.4 us (3%)
  other arithmetic  6.52 us (1%)
    pallas_call x16, Pallas kernels, run(): pl.pallas_call(body, grid_spec=pltpu.PrefetchScalarGridSpec(num_scalar_pr...  205 us
    psum x1, waiting for transfers between devices, on_device(): square = lax.psum(square, 'dp')  74.7 us
    psum x1, blocking collectives, on_device(): small = lax.psum(small, 'dp')  61.1 us
    ppermute x8, starting transfers between devices, shifted(): return lax.ppermute(block, axis, route)  14.4 us
    unnamed x58, local copies, waits for them, and re-layouts  13 us
    ppermute x8, waiting for transfers between devices, shifted(): return lax.ppermute(block, axis, route)  12.2 us
    pallas_call x1, Pallas kernels, weight_grads_ffn(): pl.pallas_call(ffn_weights, grid=(2 * blocks,), in_specs=[spec(lambda j:...  11.1 us
  transfers between devices with their start and end apart: 9, of which 3 were waited for; matrix products, arithmetic and copies ran while one was open for 1% of the time, Pallas kernels for 28%

profile of v1, /device:TPU:0, one launch (start us, length us, event | category | flops | bytes accessed | tf_op | source)
XLA Modules:
  0.0 434.1 jit_solution(13710834294979853691)
XLA Ops:
  10.7 15.1 %shard_map.246 = (bf16[3,576,512]{2,1,0:T(8,128)(2,1)}, bf16[3,64,512]{2,1,0:T(8,128)(2,1)}, bf16[3,576,512]{2,1,0:T(8,128)(2,1)}, bf16[3,576,512]{2,1,0:T(8,128...) custom-call(s32[1]{0:T(128)} %bitcast.pos_ref, ...), custom_call_target="tpu_custom_call" | custom-call | flops 1207959552 | bytes 7077888 | tf_op jit(solution)/shard_map/pallas_call | solution.py:380
  25.8 10.8 %shard_map.248 = (bf16[3,512,2048]{2,1,0:T(8,128)(2,1)}, bf16[3,512,2048]{2,1,0:T(8,128)(2,1)}, bf16[3,512,512]{2,1,0:T(8,128)(2,1)}, f32[3,512,128]{2,1,0:T(8,128)}, bf16[512,512]{1,0:T(8,128)(2,1)}) custom-call(s32[1]{0:T(128)} %bitcast.pos_ref, s32[2]{0:T(128)} %len_ref.31, bf16[3,512,512]{2,1,0:T(8,128)(2,1)} %get-tuple-element.138.refs_9_.h, ...), custom_call_target="tpu_custom_call" | custom-call | flops 2147483648 | bytes 8388608 | tf_op jit(solution)/shard_map/pallas_call | solution.py:380
  36.7 4.9 %collective-permute-start.2 = (bf16[512,512]{1,0:T(8,128)(2,1)}, bf16[512,512]{1,0:T(8,128)(2,1)S(1)}, u32[]{:S(2)}, u32[]{:S(2)}) collective-permute-start(bf16[512,512]{1,0:T(8,128)(2,1)} %get-tuple-element.149), channel_id=1, source_target_pairs={{0,16},{1,17},{2,18},{3,19},{4,20},{5,21},{6,22},{7,23},{8,24},{9,... | collective-permute-start | bytes 1572872 | tf_op jit(solution)/shard_map/ppermute | solution.py:558
  41.5 15.2 %shard_map.247 = (bf16[3,576,512]{2,1,0:T(8,128)(2,1)}, bf16[3,64,512]{2,1,0:T(8,128)(2,1)}, bf16[3,576,512]{2,1,0:T(8,128)(2,1)}, bf16[3,576,512]{2,1,0:T(8,128...) custom-call(s32[1]{0:T(128)} %bitcast.4.pos_ref, ...), custom_call_target="tpu_custom_call", output_to_operand_aliasing={{0}: (13, {}), {1}: (14, {}), {2}: (15, {}), {3}: (16, {}),... | custom-call | flops 1207959552 | bytes 7077888 | tf_op jit(solution)/shard_map/pallas_call | solution.py:380
  56.7 11.0 %shard_map.249 = (bf16[3,512,2048]{2,1,0:T(8,128)(2,1)}, bf16[3,512,2048]{2,1,0:T(8,128)(2,1)}, bf16[3,512,512]{2,1,0:T(8,128)(2,1)}, f32[3,512,128]{2,1,0:T(8,128)}, bf16[512,512]{1,0:T(8,128)(2,1)}) custom-call(s32[1]{0:T(128)} %bitcast.4.pos_ref, s32[2]{0:T(128)} %len_ref.31, ...), custom_call_target="tpu_custom_call", output_to_operand_aliasing={{0}: (10, {}), {1}: (11, {}), {2}: (12, {}), {3}: (13, {})} | custom-call | flops 2147483648 | bytes 8388608 | tf_op jit(solution)/shard_map/pallas_call | solution.py:380
  72.1 10.4 %collective-permute-done.3.mem_ref = bf16[64,512]{1,0:T(8,128)(2,1)S(1)} collective-permute-done((bf16[64,512]{1,0:T(8,128)(2,1)S(1)}, bf16[64,512]{1,0:T(8,128)(2,1)S(1)}, u32[]{:S(2)}, u32[]{:S(2)}) %collective-permute-start.3) | collective-permute-done | bytes 65568 | tf_op jit(solution)/shard_map/ppermute | solution.py:558
  83.3 15.0 %shard_map.250 = (bf16[3,576,512]{2,1,0:T(8,128)(2,1)}, bf16[3,64,512]{2,1,0:T(8,128)(2,1)}, bf16[3,576,512]{2,1,0:T(8,128)(2,1)}, bf16[3,576,512]{2,1,0:T(8,128...) custom-call(s32[1]{0:T(128)} %bitcast.1.pos_ref, ...), custom_call_target="tpu_custom_call", output_to_operand_aliasing={{0}: (13, {}), {1}: (14, {}), {2}: (15, {}), {3}: (16, {}),... | custom-call | flops 1207959552 | bytes 7077888 | tf_op jit(solution)/shard_map/pallas_call | solution.py:380
  98.3 10.9 %shard_map.252 = (bf16[3,512,2048]{2,1,0:T(8,128)(2,1)}, bf16[3,512,2048]{2,1,0:T(8,128)(2,1)}, bf16[3,512,512]{2,1,0:T(8,128)(2,1)}, f32[3,512,128]{2,1,0:T(8,128)}, bf16[512,512]{1,0:T(8,128)(2,1)}) custom-call(s32[1]{0:T(128)} %bitcast.1.pos_ref, s32[2]{0:T(128)} %len_ref.31, ...), custom_call_target="tpu_custom_call", output_to_operand_aliasing={{0}: (10, {}), {1}: (11, {}), {2}: (12, {}), {3}: (13, {})} | custom-call | flops 2147483648 | bytes 8388608 | tf_op jit(solution)/shard_map/pallas_call | solution.py:380
  110.0 15.0 %shard_map.251 = (bf16[3,576,512]{2,1,0:T(8,128)(2,1)}, bf16[3,64,512]{2,1,0:T(8,128)(2,1)}, bf16[3,576,512]{2,1,0:T(8,128)(2,1)}, bf16[3,576,512]{2,1,0:T(8,128...) custom-call(s32[1]{0:T(128)} %bitcast.3.pos_ref, ...), custom_call_target="tpu_custom_call", output_to_operand_aliasing={{0}: (13, {}), {1}: (14, {}), {2}: (15, {}), {3}: (16, {}),... | custom-call | flops 1207959552 | bytes 7077888 | tf_op jit(solution)/shard_map/pallas_call | solution.py:380
  125.0 10.8 %shard_map.253 = (bf16[3,512,2048]{2,1,0:T(8,128)(2,1)}, bf16[3,512,2048]{2,1,0:T(8,128)(2,1)}, bf16[3,512,512]{2,1,0:T(8,128)(2,1)}, f32[3,512,128]{2,1,0:T(8,128)}, bf16[512,512]{1,0:T(8,128)(2,1)}) custom-call(s32[1]{0:T(128)} %bitcast.3.pos_ref, s32[2]{0:T(128)} %len_ref.31, ...), custom_call_target="tpu_custom_call", output_to_operand_aliasing={{0}: (10, {}), {1}: (11, {}), {2}: (12, {}), {3}: (13, {})} | custom-call | flops 2147483648 | bytes 8388608 | tf_op jit(solution)/shard_map/pallas_call | solution.py:380
  135.8 9.8 %shard_map.254 = (bf16[3,512,512]{2,1,0:T(8,128)(2,1)}, bf16[3,512,2048]{2,1,0:T(8,128)(2,1)}, bf16[3,512,512]{2,1,0:T(8,128)(2,1)}, f32[512,512]{1,0:T(8,128)}, f32[16,512]{1,0:T(8,128)}) custom-call(s32[1]{0:T(128)} %bitcast.1.pos_ref, s32[2]{0:T(128)} %len_ref.31, bf16[512,512]{1,0:T(8,128)(2,1)} %get-tuple-element.279.x_ref.cot, ...), custom_call_target="tpu_custom_call" | custom-call | flops 2147483648 | bytes 8388608 | tf_op jit(solution)/shard_map/pallas_call | solution.py:380
  145.7 15.3 %shard_map.255 = (bf16[3,576,512]{2,1,0:T(8,128)(2,1)}, bf16[3,576,512]{2,1,0:T(8,128)(2,1)}, bf16[3,576,512]{2,1,0:T(8,128)(2,1)}, bf16[3,64,512]{2,1,0:T(8,128...) custom-call(s32[1]{0:T(128)} %bitcast.1.pos_ref, s32[2]{0:T(128)} %len_ref.31, ...), custom_call_target="tpu_custom_call" | custom-call | flops 1207959552 | bytes 7077888 | tf_op jit(solution)/shard_map/pallas_call | solution.py:380
  162.3 9.7 %shard_map.256 = (bf16[3,512,512]{2,1,0:T(8,128)(2,1)}, bf16[3,512,2048]{2,1,0:T(8,128)(2,1)}, bf16[3,512,512]{2,1,0:T(8,128)(2,1)}, f32[512,512]{1,0:T(8,128)}, f32[16,512]{1,0:T(8,128)}) custom-call(s32[1]{0:T(128)} %bitcast.3.pos_ref, s32[2]{0:T(128)} %len_ref.31, ...), custom_call_target="tpu_custom_call", output_to_operand_aliasing={{0}: (11, {}), {1}: (12, {}), {2}: (13, {})} | custom-call | flops 2147483648 | bytes 8388608 | tf_op jit(solution)/shard_map/pallas_call | solution.py:380
  171.9 15.4 %shard_map.258 = (bf16[3,576,512]{2,1,0:T(8,128)(2,1)}, bf16[3,576,512]{2,1,0:T(8,128)(2,1)}, bf16[3,576,512]{2,1,0:T(8,128)(2,1)}, bf16[3,64,512]{2,1,0:T(8,128...) custom-call(s32[1]{0:T(128)} %bitcast.3.pos_ref, ...), custom_call_target="tpu_custom_call", output_to_operand_aliasing={{0}: (17, {}), {1}: (18, {}), {2}: (19, {}), {3}: (20, {})} | custom-call | flops 1207959552 | bytes 7077888 | tf_op jit(solution)/shard_map/pallas_call | solution.py:380
  192.1 9.9 %shard_map.257 = (bf16[3,512,512]{2,1,0:T(8,128)(2,1)}, bf16[3,512,2048]{2,1,0:T(8,128)(2,1)}, bf16[3,512,512]{2,1,0:T(8,128)(2,1)}, f32[512,512]{1,0:T(8,128)}, f32[16,512]{1,0:T(8,128)}) custom-call(s32[1]{0:T(128)} %bitcast.pos_ref, s32[2]{0:T(128)} %len_ref.31, ...), custom_call_target="tpu_custom_call", output_to_operand_aliasing={{0}: (11, {}), {1}: (12, {}), {2}: (13, {})} | custom-call | flops 2147483648 | bytes 8388608 | tf_op jit(solution)/shard_map/pallas_call | solution.py:380
  204.4 15.5 %shard_map.259 = (bf16[3,576,512]{2,1,0:T(8,128)(2,1)}, bf16[3,576,512]{2,1,0:T(8,128)(2,1)}, bf16[3,576,512]{2,1,0:T(8,128)(2,1)}, bf16[3,64,512]{2,1,0:T(8,128...) custom-call(s32[1]{0:T(128)} %bitcast.pos_ref, ...), custom_call_target="tpu_custom_call", output_to_operand_aliasing={{0}: (17, {}), {1}: (18, {}), {2}: (19, {}), {3}: (20, {})} | custom-call | flops 1207959552 | bytes 7077888 | tf_op jit(solution)/shard_map/pallas_call | solution.py:380
  220.8 9.6 %shard_map.260 = (bf16[3,512,512]{2,1,0:T(8,128)(2,1)}, bf16[3,512,2048]{2,1,0:T(8,128)(2,1)}, bf16[3,512,512]{2,1,0:T(8,128)(2,1)}, f32[512,512]{1,0:T(8,128)}, f32[16,512]{1,0:T(8,128)}) custom-call(s32[1]{0:T(128)} %bitcast.4.pos_ref, s32[2]{0:T(128)} %len_ref.31, ...), custom_call_target="tpu_custom_call", output_to_operand_aliasing={{0}: (11, {}), {1}: (12, {}), {2}: (13, {})} | custom-call | flops 2147483648 | bytes 8388608 | tf_op jit(solution)/shard_map/pallas_call | solution.py:380
  230.4 11.1 %shard_map.263 = bf16[8,512,512]{2,1,0:T(8,128)(2,1)} custom-call(bf16[3,512,2048]{2,1,0:T(8,128)(2,1)} %get-tuple-element.242.g, bf16[3,512,512]{2,1,0:T(8,128)(2,1)} %get-tuple-element.243.gd, bf16[3,512,512]{2,1,0:T(8,128)(2,1)} %get-tuple-element.172.h, bf16[3,512,2048]{2,1,0:T(8,128)(2,1)} %get-tuple-element.244.gf), custom_call_target="tpu_custom_call" | custom-call | flops 4294967296 | bytes 12582912 | tf_op jit(solution)/shard_map/pallas_call | solution.py:508
  242.2 15.5 %shard_map.261 = (bf16[3,576,512]{2,1,0:T(8,128)(2,1)}, bf16[3,576,512]{2,1,0:T(8,128)(2,1)}, bf16[3,576,512]{2,1,0:T(8,128)(2,1)}, bf16[3,64,512]{2,1,0:T(8,128...) custom-call(s32[1]{0:T(128)} %bitcast.4.pos_ref, ...), custom_call_target="tpu_custom_call", output_to_operand_aliasing={{0}: (17, {}), {1}: (18, {}), {2}: (19, {}), {3}: (20, {})} | custom-call | flops 1207959552 | bytes 7077888 | tf_op jit(solution)/shard_map/pallas_call | solution.py:380
  257.7 8.3 %shard_map.262 = bf16[4,512,512]{2,1,0:T(8,128)(2,1)} custom-call(bf16[3,576,512]{2,1,0:T(8,128)(2,1)} %get-tuple-element.235.uc, bf16[3,64,512]{2,1,0:T(8,128)(2,1)} %get-tuple-element.236.mem, bf16[3,576,512]{2,1,0:T(8,128)(2,1)} %get-tuple-element.237.mix, bf16[3,576,512]{2,1,0:T(8,128)(2,1)} %get-tuple-element.238.gq, ...), custom_call_target="tpu_custom_call" | custom-call | flops 2415919104 | bytes 9437184 | tf_op jit(solution)/shard_map/pallas_call | solution.py:544
  267.0 61.1 %psum.21 = f32[14,512]{1,0:T(8,128)S(1)} all-reduce(f32[14,512]{1,0:T(8,128)S(1)} %concatenate.4), channel_id=1, replica_groups=mesh['section'=2,'dp'=16] {'dp'}, use_global_device_ids=true, to_apply=%region_0.1 | all-reduce | flops 7168 | bytes 57344 | tf_op jit(solution)/shard_map/psum | solution.py:618
  332.3 74.7 %all-reduce.3.cloned.1.call-done = (bf16[4,512,512]{2,1,0:T(8,128)(2,1)}, bf16[8,512,512]{2,1,0:T(8,128)(2,1)}) async-done(((bf16[4,512,512]{2,1,0:T(8,128)(2,1)}, bf16[8,512,512]{2,1,0:T(8,128)(2,1)}), (bf16[4,512,512]{2,1,0:T(8,128)(2,1)}, bf16[8,512,512]{2,1,0:T(8,128)(2,1)})) %all-reduce.3.cloned.1.call-update) | async-done | bytes 6291472 | tf_op jit(solution)/shard_map/psum | solution.py:608
  416.2 5.2 %copy.96 = f32[512,4,512]{0,2,1:T(8,128)} copy(f32[512,4,512]{2,0,1:T(8,128)} %get-tuple-element.274) | data formatting | bytes 8388608 | tf_op jit(solution)/shard_map/reshape | solution.py:622
  421.5 5.3 %copy.99 = f32[1,512,2048]{2,1,0:T(8,128)} copy(f32[1,512,2048]{1,2,0:T(8,128)} %bitcast.89) | data formatting | bytes 8388608
  (88 shorter events, 33.7 us)
Async XLA Ops:
  7.2 2.3 copy-start.21
  7.2 2.3 copy-start.22
  7.2 399.8 %all-reduce.3.cloned.1.call-start = ((), (), s32[]{:S(2)}) async-start(), calls=%async_computation | async-start | bytes 12582912 | tf_op jit(solution)/shard_map/psum | solution.py:608
  36.7 45.8 %collective-permute-start.2 = (bf16[512,512]{1,0:T(8,128)(2,1)}, bf16[512,512]{1,0:T(8,128)(2,1)S(1)}, u32[]{:S(2)}, u32[]{:S(2)}) collective-permute-start(bf16[512,512]{1,0:T(8,128)(2,1)} %get-tuple-element.149), channel_id=1, source_target_pairs={{0,16},{1,17},{2,18},{3,19},{4,20},{5,21},{6,22},{7,23},{8,24},{9,... | collective-permute-start | bytes 1572872 | tf_op jit(solution)/shard_map/ppermute | solution.py:558
  56.7 12.3 %copy-start.24 = (bf16[64,512]{1,0:T(8,128)(2,1)S(1)}, bf16[64,512]{1,0:T(8,128)(2,1)}, u32[]{:S(2)}) copy-start(bf16[64,512]{1,0:T(8,128)(2,1)} %get-tuple-element.150) | copy-start | bytes 196612
  56.7 13.6 %copy-start.23 = (bf16[64,512]{1,0:T(8,128)(2,1)S(1)}, bf16[64,512]{1,0:T(8,128)(2,1)}, u32[]{:S(2)}) copy-start(bf16[64,512]{1,0:T(8,128)(2,1)} %get-tuple-element.148) | copy-start | bytes 196612
  67.7 41.5 %collective-permute-start = (bf16[512,512]{1,0:T(8,128)(2,1)}, bf16[512,512]{1,0:T(8,128)(2,1)S(1)}, u32[]{:S(2)}, u32[]{:S(2)}) collective-permute-start(bf16[512,512]{1,0:T(8,128)(2,1)} %get-tuple-element.147), channel_id=1, source_target_pairs={{0,16},{1,17},{2,18},{3,19},{4,20},{5,21},{6,22},{7,23},{8,24},{9,... | collective-permute-start | bytes 1572872 | tf_op jit(solution)/shard_map/ppermute | solution.py:558
  69.0 13.4 %collective-permute-start.3 = (bf16[64,512]{1,0:T(8,128)(2,1)S(1)}, bf16[64,512]{1,0:T(8,128)(2,1)S(1)}, u32[]{:S(2)}, u32[]{:S(2)}) collective-permute-start(bf16[64,512]{1,0:T(8,128)(2,1)S(1)} %copy-done.24), channel_id=1, source_target_pairs={{0,16},{1,17},{2,18},{3,19},{4,20},{5,21},{6,22},{7,23},{8,24},{9,... | collective-permute-start | bytes 196616 | tf_op jit(solution)/shard_map/ppermute | solution.py:558
  70.3 38.8 %collective-permute-start.1 = (bf16[64,512]{1,0:T(8,128)(2,1)S(1)}, bf16[64,512]{1,0:T(8,128)(2,1)S(1)}, u32[]{:S(2)}, u32[]{:S(2)}) collective-permute-start(bf16[64,512]{1,0:T(8,128)(2,1)S(1)} %copy-done.23), channel_id=1, source_target_pairs={{0,16},{1,17},{2,18},{3,19},{4,20},{5,21},{6,22},{7,23},{8,24},{9,... | collective-permute-start | bytes 196616 | tf_op jit(solution)/shard_map/ppermute | solution.py:558
  82.5 0.8 copy-start.2
  109.2 0.8 copy-start.1
  161.0 30.3 %collective-permute-start.4 = (bf16[512,512]{1,0:T(8,128)(2,1)}, bf16[512,512]{1,0:T(8,128)(2,1)S(1)}, u32[]{:S(2)}, u32[]{:S(2)}) collective-permute-start(bf16[512,512]{1,0:T(8,128)(2,1)} %get-tuple-element.195), channel_id=1, source_target_pairs={{16,0},{17,1},{18,2},{19,3},{20,4},{21,5},{22,6},{23,7},{24,8},{25... | collective-permute-start | bytes 1572872 | tf_op jit(solution)/shard_map/ppermute | solution.py:558
  171.9 16.7 %copy-start.25 = (bf16[64,512]{1,0:T(8,128)(2,1)S(1)}, bf16[64,512]{1,0:T(8,128)(2,1)}, u32[]{:S(2)}) copy-start(bf16[64,512]{1,0:T(8,128)(2,1)} %get-tuple-element.202) | copy-start | bytes 196612
  187.4 32.6 %collective-permute-start.6 = (bf16[512,512]{1,0:T(8,128)(2,1)}, bf16[512,512]{1,0:T(8,128)(2,1)S(1)}, u32[]{:S(2)}, u32[]{:S(2)}) collective-permute-start(bf16[512,512]{1,0:T(8,128)(2,1)} %get-tuple-element.214), channel_id=1, source_target_pairs={{16,0},{17,1},{18,2},{19,3},{20,4},{21,5},{22,6},{23,7},{24,8},{25... | collective-permute-start | bytes 1572872 | tf_op jit(solution)/shard_map/ppermute | solution.py:558
  188.7 15.1 %collective-permute-start.5 = (bf16[64,512]{1,0:T(8,128)(2,1)S(1)}, bf16[64,512]{1,0:T(8,128)(2,1)S(1)}, u32[]{:S(2)}, u32[]{:S(2)}) collective-permute-start(bf16[64,512]{1,0:T(8,128)(2,1)S(1)} %copy-done.25), channel_id=1, source_target_pairs={{16,0},{17,1},{18,2},{19,3},{20,4},{21,5},{22,6},{23,7},{24,8},{25... | collective-permute-start | bytes 196616 | tf_op jit(solution)/shard_map/ppermute | solution.py:558
  190.0 51.6 %collective-permute-start.7 = (bf16[64,512]{1,0:T(8,128)(2,1)}, bf16[64,512]{1,0:T(8,128)(2,1)S(1)}, u32[]{:S(2)}, u32[]{:S(2)}) collective-permute-start(bf16[64,512]{1,0:T(8,128)(2,1)} %get-tuple-element.218), channel_id=1, source_target_pairs={{16,0},{17,1},{18,2},{19,3},{20,4},{21,5},{22,6},{23,7},{24,8},{25... | collective-permute-start | bytes 196616 | tf_op jit(solution)/shard_map/ppermute | solution.py:558
  266.1 0.8 copy-start.13
  266.1 0.8 copy-start.17
  266.1 0.8 copy-start.19
  266.1 63.8 %copy-start.5 = (bf16[512,512]{1,0:T(8,128)(2,1)S(1)}, bf16[512,512]{1,0:T(8,128)(2,1)}, u32[]{:S(2)}) copy-start(bf16[512,512]{1,0:T(8,128)(2,1)} %get-tuple-element.225) | copy-start | bytes 1572868
  266.1 63.8 %copy-start.6 = (bf16[512,512]{1,0:T(8,128)(2,1)S(1)}, bf16[512,512]{1,0:T(8,128)(2,1)}, u32[]{:S(2)}) copy-start(bf16[512,512]{1,0:T(8,128)(2,1)} %get-tuple-element.226) | copy-start | bytes 1572868
  266.1 63.8 %copy-start.7 = (bf16[512,512]{1,0:T(8,128)(2,1)S(1)}, bf16[512,512]{1,0:T(8,128)(2,1)}, u32[]{:S(2)}) copy-start(bf16[512,512]{1,0:T(8,128)(2,1)} %get-tuple-element.213) | copy-start | bytes 1572868
  266.1 63.8 %copy-start.8 = (bf16[512,512]{1,0:T(8,128)(2,1)S(1)}, bf16[512,512]{1,0:T(8,128)(2,1)}, u32[]{:S(2)}) copy-start(bf16[512,512]{1,0:T(8,128)(2,1)} %get-tuple-element.224) | copy-start | bytes 1572868
  407.0 3.9 copy-start
  (11 other events, 8.0 us)
Sparse Core Ops, SparseCore 0:
  266.3 140.6 all-reduce.2
